TPU v7x, 256 devices: a whole 4x4x8 slice. The times are simulated.
256 devices in a mesh: lon: 8 (over x_hi, y), lat: 32 (over x_lo, z, core).
Axes of the slice: x: 4 (x_hi: 2, x_lo: 2; x = x_hi * 2 + x_lo), y: 4, z: 8, core: 2. Of those that a mesh axis runs over, the one named last changes fastest.
Arguments:
- tracer: float32 [8, 1536, 1024], P(None, 'lat', 'lon'), may hold values from -6 to 6
- salinity: float32 [8, 1536, 1024], P(None, 'lat', 'lon'), may hold values from -6 to 6
- zonal_vel: float32 [8, 1536, 1024], P(None, 'lat', 'lon'), may hold values from -4 to 4
- merid_vel: float32 [8, 1536, 1024], P(None, 'lat', 'lon'), may hold values from -4 to 4
- surface: float32 [1536, 1024], P('lat', 'lon'), may hold values from -6 to 6
- land_mask: int32 [8, 1536, 1024], P(None, 'lat', 'lon'), may hold values 0 or 1
- bottom_level: int32 [1536, 1024], P('lat', 'lon'), may hold values from 7 to 8
- tracer_adj: float32 [8, 1536, 1024], P(None, 'lat', 'lon'), may hold values from -6 to 6
- salinity_adj: float32 [8, 1536, 1024], P(None, 'lat', 'lon'), may hold values from -6 to 6
- zonal_adj: float32 [8, 1536, 1024], P(None, 'lat', 'lon'), may hold values from -6 to 6
- merid_adj: float32 [8, 1536, 1024], P(None, 'lat', 'lon'), may hold values from -6 to 6
- surface_adj: float32 [1536, 1024], P('lat', 'lon'), may hold values from -6 to 6
- stream_adj: float32 [1536, 1024], P('lat', 'lon'), may hold values from -0.625 to 0.625
Outputs:
- tracer_grad: float32 [8, 1536, 1024], P(None, 'lat', 'lon')
- salinity_grad: float32 [8, 1536, 1024], P(None, 'lat', 'lon')
- zonal_grad: float32 [8, 1536, 1024], P(None, 'lat', 'lon')
- merid_grad: float32 [8, 1536, 1024], P(None, 'lat', 'lon')
- surface_grad: float32 [1536, 1024], P('lat', 'lon')
All inputs are finite; a program needn't handle non-finite values. No bound on the sum of `land_mask` on one device may be relied on, other than what follows from the above.
Results may differ from a plain program's by a relative error of at most 0.00002.
Values sent between devices are 32-bit elements; how exact they have to be, the bound alone decides.
A program may use at most 64 MiB of HBM per device.

v0:
```python
import jax
import jax.numpy as jnp
from jax import lax
from jax.experimental import pallas as pl
from jax.experimental.pallas import tpu as pltpu
from jax.sharding import PartitionSpec as P

MESH = pl.DeviceIdType.MESH
F32 = jnp.float32
SUBCYCLES = 8
LEVELS = 8
ROWS = 48
LANES = 128
HALO = 16

ADVECT = 0.25
DIFFUSION = 0.1
HEAT_COEF = 0.5
SALT_COEF = 0.4
PRESS_COEF = 0.3
CORIOLIS = 0.3
DRAG_COEF = 0.5
DIVERGENCE = 0.5
SLOPE_COEF = 0.5
FRICTION = 0.05
THICK_COEF = 0.3

CT, CS, WU, WV, WET, AT, AS, WZ, WM = range(9)
OWN = slice(16, 64)
ZR = slice(16, 72)
MR = slice(8, 64)
TALL = 80
BODY = slice(8, 88)
MINE = slice(24, 72)
WIDE = 96
SF_H, SF_HADJ, SF_WT, SF_U, SF_V, SF_FU, SF_FV, SF_CU, SF_CV, SF_SU, SF_SV = range(11)
SIDES = ((1, 0), (-1, 0), (0, 1), (0, -1), (1, 1), (-1, 1), (1, -1), (-1, -1))


def roll(x, shift):
    return pltpu.roll(x, shift, axis=x.ndim - 1)


def lanes_of(rows):
    return lax.broadcasted_iota(jnp.int32, (rows, LANES), 1)


def pair_east(a, b):
    last = lanes_of(a.shape[0]) == LANES - 1
    ra, rb = roll(a, LANES - 1), roll(b, LANES - 1)
    return jnp.where(last, rb, ra), jnp.where(last, ra, rb)


def pair_west(a, b):
    first = lanes_of(a.shape[0]) == 0
    ra, rb = roll(a, 1), roll(b, 1)
    return jnp.where(first, rb, ra), jnp.where(first, ra, rb)


def kernel(
    nlon, nlat, inner,
    tracer, salinity, zonal, merid, surface, mask, bottom, tr_adj, sa_adj, zo_adj, me_adj, su_adj, st_adj,
    out_t, out_s, out_u, out_v, out_h,
    x, lm, bl, stv, c1, pw1, pe1, m1, rn, rs, got_s, got_n, tot, slot1, gsum, slot2, sfx,
    um0, umw, vm0, we, wew, wn, z1, z1w, mm1, mm1e, wne, tmp3, sut, svt,
    acc, acx, c2, pw2, pe2, m2, sa, sb, st, ou2, cd2, wt2, ff2, ga, gb, fg, tmpb, gg,
    in_sem, send_sem, recv_sem,
):
    lon, lat = lax.axis_index("lon"), lax.axis_index("lat")
    outer = nlat // inner

    def at(dlon, dlat):
        return (lax.rem(lon + dlon + nlon, nlon), lax.rem(lat + dlat + nlat, nlat))

    loads = []
    for src, dst in (
        (mask, lm), (bottom, bl), (st_adj, stv),
        (tracer, x.at[CT, :, OWN]), (salinity, x.at[CS, :, OWN]), (zonal, x.at[WU, :, OWN]), (merid, x.at[WV, :, OWN]),
        (tr_adj, x.at[AT, :, OWN]), (sa_adj, x.at[AS, :, OWN]), (zo_adj, x.at[WZ, :, OWN]), (me_adj, x.at[WM, :, OWN]),
        (surface, sa.at[SF_H, MINE]), (su_adj, sa.at[SF_HADJ, MINE]),
    ):
        copy = pltpu.make_async_copy(src, dst, in_sem.at[len(loads)])
        copy.start()
        loads.append(copy)

    gi, go = lax.rem(lat, inner), lat // inner
    mates = [(lon, go * inner + lax.rem(gi + d, inner)) for d in range(1, inner)]
    peers = [(lon, lax.rem(go + e, outer) * inner + gi) for e in range(1, outer)]
    around = [at(*side) for side in SIDES]

    barrier = pltpu.get_barrier_semaphore()
    for where in around + mates + peers:
        pl.semaphore_signal(barrier, inc=1, device_id=where, device_id_type=MESH)

    sent = []

    def send(src, dst, where):
        n = len(sent)
        copy = pltpu.make_async_remote_copy(
            src_ref=src, dst_ref=dst, send_sem=send_sem.at[n], recv_sem=recv_sem.at[n],
            device_id=where, device_id_type=MESH,
        )
        copy.start()
        sent.append(copy)
        return copy

    for copy in loads[:3]:
        copy.wait()
    pad = jnp.zeros((8, LANES), F32)
    tile_sum = stv[0:8]
    for r in range(1, ROWS // 8):
        tile_sum = tile_sum + stv[8 * r : 8 * r + 8]
    tot[...] = tile_sum
    pl.semaphore_wait(barrier, len(around) + len(mates) + len(peers))
    up1 = [send(tot, slot1.at[d - 1], mates[d - 1]) for d in range(1, inner)]

    for copy in loads[3:]:
        copy.wait()

    lane = lanes_of(ROWS)

    def mask_level(k, _):
        bottoms = bl[...]
        wet = jnp.where((lm[k] > 0) & (k < bottoms), 1.0, 0.0).astype(F32)
        packs = [c1[0], c1[1], c1[2]]
        for f in range(9):
            if f == WET:
                value = wet
            else:
                value = x[f, k, OWN] * wet
            x[f, k, OWN] = value
            here = lax.shift_right_logical(lane, 2) == 8 * (f % 4) + k
            packs[f // 4] = jnp.where(here, roll(value, 32 * (f % 4) + 4 * k + 2), packs[f // 4])
        for n in range(3):
            c1[n] = packs[n]
        return 0

    lax.fori_loop(0, LEVELS, mask_level, 0)

    def pack_rows(f, _):
        for k in range(LEVELS):
            rs[f, 2 * k : 2 * k + 2] = x[f, k, 16:18]
            rn[f, 2 * k : 2 * k + 2] = x[f, k, 62:64]
        return 0

    lax.fori_loop(0, 9, pack_rows, 0)
    sa[SF_WT, MINE] = x[WET, 0, OWN]
    pack = c1[2]
    for s, f in ((1, SF_H), (2, SF_HADJ), (3, SF_WT)):
        here = lax.shift_right_logical(lane, 5) == s
        pack = jnp.where(here, roll(sa[f, MINE], (32 * s + 16) % LANES), pack)
    c1[2] = pack

    LOW, HIGH = slice(0, 16), slice(32, 48)

    def exchange(c, pw, pe, first, last):
        return [
            send(c, pw.at[:, 16:64], around[0]),
            send(c, pe.at[:, 16:64], around[1]),
            send(sa.at[first:last, 56:72], sa.at[first:last, 8:24], around[2]),
            send(sa.at[first:last, 24:40], sa.at[first:last, 72:88], around[3]),
            send(c.at[:, HIGH], pw.at[:, 0:16], around[4]),
            send(c.at[:, HIGH], pe.at[:, 0:16], around[5]),
            send(c.at[:, LOW], pw.at[:, 64:80], around[6]),
            send(c.at[:, LOW], pe.at[:, 64:80], around[7]),
        ]

    phase1 = [send(rn, got_s, around[2]), send(rs, got_n, around[3])]
    phase1 += exchange(c1, pw1, pe1, 0, 3)

    sfx[0:48] = stv[...]
    for r in range(6):
        sfx[48 + 8 * r : 56 + 8 * r] = pad
    for step in (1, 2, 4, 8, 16, 32):
        moved = sfx[0:48] + sfx[step : step + 48]
        sfx[0:48] = moved
    for n in range(3):
        for p in range(2):
            st[n, p, 0:8] = pad
            st[n, p, 88:96] = pad
    for p in range(2):
        tmpb[p, 0:8] = pad
        tmpb[p, 88:96] = pad
    acc[...] = jnp.zeros_like(acc)
    acx[...] = jnp.zeros_like(acx)

    for copy in up1:
        copy.wait_recv()
    group = tot[...]
    above = jnp.zeros((8, LANES), F32)
    for d in range(1, inner):
        got = slot1[d - 1]
        group = group + got
        above = above + jnp.where(lax.rem(gi - d + inner, inner) > gi, got, 0.0)
    gsum[...] = group
    up2 = [send(gsum, slot2.at[e - 1], peers[e - 1]) for e in range(1, outer)]

    for copy in phase1:
        copy.wait_recv()
    south_here, north_here = lat > 0, lat < nlat - 1

    def unpack_rows(f, _):
        for k in range(LEVELS):
            x[f, k, 14:16] = jnp.where(south_here, got_s[f, 2 * k : 2 * k + 2], 0.0)
            x[f, k, 64:66] = jnp.where(north_here, got_n[f, 2 * k : 2 * k + 2], 0.0)
        return 0

    lax.fori_loop(0, 9, unpack_rows, 0)
    lane80 = lanes_of(80)
    rows80 = lax.broadcasted_iota(jnp.int32, (80, LANES), 0)
    inside = ((rows80 >= 16) | south_here) & ((rows80 < 64) | north_here)
    fine = (lane80 & 3) < 2
    coarse = (lane80 & 31) < 16
    for n in range(3):
        from_west = fine if n < 2 else jnp.where(lane80 < 32, fine.astype(jnp.int32), coarse.astype(jnp.int32)) > 0
        m1[n] = jnp.where(inside, jnp.where(from_west, pw1[n], pe1[n]), 0.0)

    def strip(f, k, rows):
        return roll(m1[f // 4, rows], 126 - 32 * (f % 4) - 4 * k)

    def shifted(value, rim, offset):
        ids = lanes_of(value.shape[0])
        if offset > 0:
            return roll(jnp.where(ids < offset, rim, value), LANES - offset)
        return roll(jnp.where(ids >= LANES + offset, rim, value), -offset)

    row_ids = lax.broadcasted_iota(jnp.int32, (64, LANES), 0) + (lat * ROWS - 8)
    cor = -(1.0 + row_ids.astype(F32) / (ROWS * nlat))

    EXT = slice(8, 72)

    def forward_level(k, _):
        wet = x[WET, k, EXT]
        wet_e = shifted(wet, strip(WET, k, EXT), 1)
        tmp3[EXT] = wet_e
        wet_n = x[WET, k, 9:73]
        east, north = wet * wet_e, wet * wet_n
        we[k, EXT] = east
        wn[k, EXT] = north
        wu, wv = x[WU, k, EXT], x[WV, k, EXT]
        u0 = wu * wet_e
        v0 = wv * wet_n
        uw = shifted(wu, strip(WU, k, EXT), -1) * wet
        ve = shifted(wv, strip(WV, k, EXT), 1) * tmp3[9:73]
        um0[k, EXT] = u0
        umw[k, EXT] = uw
        vm0[k, EXT] = v0
        sut[EXT] = u0 + uw
        svt[EXT] = v0 + ve
        zz = x[WZ, k, EXT] * wet_e
        mz = x[WM, k, EXT] * wet_n
        z1[k, EXT] = zz
        mm1[k, EXT] = mz
        acx[0] = acx[0] + zz
        acx[1] = acx[1] + east
        acx[2] = acx[2] + mz
        acx[3] = acx[3] + north

        t0 = SALT_COEF * x[CS, k, OWN] - HEAT_COEF * x[CT, k, OWN]
        tn = SALT_COEF * x[CS, k, 17:65] - HEAT_COEF * x[CT, k, 17:65]
        te = shifted(t0, SALT_COEF * strip(CS, k, OWN) - HEAT_COEF * strip(CT, k, OWN), 1)
        dpe = acc[4] + (te - t0)
        dpn = acc[5] + (tn - t0)
        acc[4] = dpe
        acc[5] = dpn
        own = slice(8, 56)
        drag = jnp.where(bl[...] - 1 == k, 1.0 - DRAG_COEF, 1.0)
        uo, vo = u0[own], v0[own]
        vu = (0.25 * CORIOLIS) * cor[own] * (svt[OWN] + svt[15:63])
        uv = (0.25 * CORIOLIS) * cor[own] * (sut[OWN] + sut[17:65])
        zn = uo * drag + east[own] * (vu - (PRESS_COEF / LEVELS) * dpe)
        mn = vo * drag - north[own] * (uv + (PRESS_COEF / LEVELS) * dpn)
        acc[0] = acc[0] + uo
        acc[1] = acc[1] + vo
        acc[2] = acc[2] + zn
        acc[3] = acc[3] + mn
        return 0

    tmp3[72:80] = pad
    lax.fori_loop(0, LEVELS, forward_level, 0)

    for copy in up2:
        copy.wait_recv()
    for e in range(1, outer):
        got = slot2[e - 1]
        above = above + jnp.where(lax.rem(go - e + outer, outer) > go, got, 0.0)
    above = jnp.sum(above, axis=0, keepdims=True)

    def over(num, count):
        return num / jnp.maximum(count, 1.0)

    own = slice(8, 56)
    cu, cv = acx[1, own], acx[3, own]
    surf = [
        acc[0] / LEVELS, acc[1] / LEVELS,
        (acc[2] - acc[0]) / (LEVELS * SUBCYCLES), (acc[3] - acc[1]) / (LEVELS * SUBCYCLES),
        cu, cv,
        LEVELS * over(acx[0, own], cu) + (sfx[0:48] + above),
        LEVELS * over(acx[2, own], cv),
    ]
    for n in range(2):
        pack = None
        for s in range(4):
            value = surf[4 * n + s]
            sa[SF_U + 4 * n + s, MINE] = value
            turned = roll(value, (32 * s + 16) % LANES)
            pack = turned if s == 0 else jnp.where(lax.shift_right_logical(lane, 5) == s, turned, pack)
        c2[n] = pack
    phase2 = exchange(c2, pw2, pe2, 3, 11)

    def advect_level(k, _):
        wet_rim = strip(WET, k, OWN)
        wet = x[WET, k, OWN]
        u_rim, wu = strip(WU, k, OWN), x[WU, k, OWN]
        u0, u_w = um0[k, OWN], umw[k, OWN]
        u_ww = shifted(wu, u_rim, -2) * shifted(wet, wet_rim, -1)
        u_e = shifted(wu, u_rim, 1) * shifted(wet, wet_rim, 2)
        we0, we_w = we[k, OWN], wet * shifted(wet, wet_rim, -1)
        v0, v_s, v_ss, v_n = vm0[k, OWN], vm0[k, 15:63], vm0[k, 14:62], vm0[k, 17:65]
        wn0, wn_s = wn[k, OWN], wn[k, 15:63]
        grad_u = jnp.zeros((ROWS, LANES), F32)
        grad_v = jnp.zeros((ROWS, LANES), F32)
        for c, a, out in ((CT, AT, out_t), (CS, AS, out_s)):
            a0, a_rim = x[a, k, OWN], strip(a, k, OWN)
            c0, c_rim = x[c, k, OWN], strip(c, k, OWN)
            a_e, a_ee = shifted(a0, a_rim, 1), shifted(a0, a_rim, 2)
            a_w, a_ww = shifted(a0, a_rim, -1), shifted(a0, a_rim, -2)
            d0, d_w, d_ww, d_e = a_e - a0, a0 - a_w, a_w - a_ww, a_ee - a_e
            c_e, c_ee, c_w = shifted(c0, c_rim, 1), shifted(c0, c_rim, 2), shifted(c0, c_rim, -1)
            grad_u = grad_u + d0 * ((ADVECT * 7.0 / 12.0) * (c0 + c_e) - (ADVECT / 12.0) * (c_w + c_ee))
            grad = a0 + (ADVECT * 7.0 / 12.0) * (u0 * d0 + u_w * d_w) - (ADVECT / 12.0) * (u_e * d_e + u_ww * d_ww)
            grad = grad + DIFFUSION * (we0 * d0 - we_w * d_w)
            a_n, a_nn, a_s, a_ss = x[a, k, 17:65], x[a, k, 18:66], x[a, k, 15:63], x[a, k, 14:62]
            d0, d_s, d_ss, d_n = a_n - a0, a0 - a_s, a_s - a_ss, a_nn - a_n
            c_n, c_nn, c_s = x[c, k, 17:65], x[c, k, 18:66], x[c, k, 15:63]
            grad_v = grad_v + d0 * ((ADVECT * 7.0 / 12.0) * (c0 + c_n) - (ADVECT / 12.0) * (c_s + c_nn))
            grad = grad + (ADVECT * 7.0 / 12.0) * (v0 * d0 + v_s * d_s) - (ADVECT / 12.0) * (v_n * d_n + v_ss * d_ss)
            grad = grad + DIFFUSION * (wn0 * d0 - wn_s * d_s)
            out[k] = grad
        out_u[k] = grad_u
        out_v[k] = grad_v
        wet_x = x[WET, k, EXT]
        rim_x = strip(WET, k, EXT)
        wet_ex = shifted(wet_x, rim_x, 1)
        tmp3[EXT] = wet_ex
        wet_en = tmp3[9:73]
        east_w = wet_x * shifted(wet_x, rim_x, -1)
        north_e = wet_ex * wet_en
        z_w = shifted(x[WZ, k, EXT], strip(WZ, k, EXT), -1) * wet_x
        m_e = shifted(x[WM, k, EXT], strip(WM, k, EXT), 1) * wet_en
        wew[k, EXT] = east_w
        wne[k, EXT] = north_e
        z1w[k, EXT] = z_w
        mm1e[k, EXT] = m_e
        acx[4] = acx[4] + z_w
        acx[5] = acx[5] + east_w
        acx[6] = acx[6] + m_e
        acx[7] = acx[7] + north_e
        return 0

    lax.fori_loop(0, LEVELS, advect_level, 0)

    for copy in phase2:
        copy.wait_recv()

    rim_lane = (lane80 < HALO) | (lane80 >= LANES - HALO)
    for n in range(2):
        m2[n] = jnp.where(inside, jnp.where(coarse, pw2[n], pe2[n]), 0.0)
    for f in range(11):
        source, s = (m1[2], f + 1) if f < 3 else (m2[(f - 3) // 4], (f - 3) % 4)
        sb[f] = jnp.where(rim_lane, roll(source, (LANES - 16 - 32 * s) % LANES), 0.0)

    def part(f, p):
        return jnp.where(inside, sa[f, BODY], 0.0) if p == 0 else sb[f]

    for p in range(2):
        st[0, p, BODY] = part(SF_H, p)
        st[1, p, BODY] = part(SF_U, p)
        st[2, p, BODY] = part(SF_V, p)
        wt2[p] = part(SF_WT, p)
        for d in range(2):
            count = part(SF_CU + d, p)
            opened = jnp.minimum(count, 1.0)
            ou2[d, p] = opened
            cd2[d, p] = (SLOPE_COEF / LEVELS) * count
            ff2[d, p] = opened * part(SF_FU + d, p)
            fg[d, p] = jnp.zeros((80, LANES), F32)

    BOTH = (0, 1)

    def sub_step(n, _):
        u = [st[1, p, BODY] for p in BOTH]
        v = [st[2, p, BODY] for p in BOTH]
        u_w = pair_west(*u)
        h = [
            wt2[p] * (st[0, p, BODY] - DIVERGENCE * ((u[p] - u_w[p]) + (v[p] - st[2, p, 7:87])))
            for p in BOTH
        ]
        for p in BOTH:
            st[0, p, BODY] = h[p]
        h_e = pair_east(*h)
        for p in BOTH:
            for d, old, far in ((0, u[p], h_e[p]), (1, v[p], st[0, p, 9:89])):
                slope = far - h[p]
                bend = jnp.tanh(0.5 * (h[p] + far))
                depth = cd2[d, p]
                level = depth * (1.0 + THICK_COEF * bend)
                tilt = depth * (0.5 * THICK_COEF) * (1.0 - bend * bend) * slope
                ga[n, d, p] = level - tilt
                gb[n, d, p] = level + tilt
                st[1 + d, p, BODY] = (1.0 - FRICTION) * ou2[d, p] * old + ff2[d, p] - level * slope
        return 0

    lax.fori_loop(0, SUBCYCLES, sub_step, 0)

    for p in BOTH:
        st[0, p, BODY] = part(SF_HADJ, p)
        st[1, p, BODY] = part(SF_SU, p)
        st[2, p, BODY] = part(SF_SV, p)

    def back_step(i, _):
        n = SUBCYCLES - 1 - i
        u = [ou2[0, p] * st[1, p, BODY] for p in BOTH]
        v = [ou2[1, p] * st[2, p, BODY] for p in BOTH]
        for p in BOTH:
            fg[0, p] = fg[0, p] + u[p]
            fg[1, p] = fg[1, p] + v[p]
            tmpb[p, BODY] = gb[n, 1, p] * v[p]
        b_w = pair_west(*[gb[n, 0, p] * u[p] for p in BOTH])
        h = [
            wt2[p] * (st[0, p, BODY] + (ga[n, 0, p] * u[p] - b_w[p]) + (ga[n, 1, p] * v[p] - tmpb[p, 7:87]))
            for p in BOTH
        ]
        for p in BOTH:
            st[0, p, BODY] = h[p]
        h_e = pair_east(*h)
        for p in BOTH:
            st[1, p, BODY] = (1.0 - FRICTION) * u[p] - DIVERGENCE * (h[p] - h_e[p])
            st[2, p, BODY] = (1.0 - FRICTION) * v[p] - DIVERGENCE * (h[p] - st[0, p, 9:89])
        return 0

    lax.fori_loop(0, SUBCYCLES, back_step, 0)

    out_h[...] = st[0, 0, MINE]
    window = slice(8, 72)
    force = 1.0 / (LEVELS * SUBCYCLES)
    fu, fv = fg[0, 0], fg[1, 0]
    fu_w = pair_west(fu, fg[0, 1])[0]
    fv_e = pair_east(fv, fg[1, 1])[0]
    gg[0] = force * fu[window] - over(acx[0], acx[1])
    gg[1] = force * fu_w[window] - over(acx[4], acx[5])
    gg[2] = force * fv[window] - over(acx[2], acx[3])
    gg[3] = force * fv_e[window] - over(acx[6], acx[7])
    acc[0] = (st[1, 0, MINE] - fu[16:64] / SUBCYCLES) / LEVELS
    acc[1] = (st[2, 0, MINE] - fv[16:64] / SUBCYCLES) / LEVELS

    turn = (0.25 * CORIOLIS) * cor

    def momentum_level(i, press):
        k = LEVELS - 1 - i
        z = z1[k, ZR] + we[k, ZR] * gg[0, 8:64]
        z_w = z1w[k, ZR] + wew[k, ZR] * gg[1, 8:64]
        m = mm1[k, MR] + wn[k, MR] * gg[2, 0:56]
        m_e = mm1e[k, MR] + wne[k, MR] * gg[3, 0:56]
        sut[ZR] = turn[8:64] * (z + z_w)
        svt[MR] = turn[0:56] * (m + m_e)
        tmp3[MR] = m
        z0, m0 = z[0:48], m[8:56]
        press = press + (PRESS_COEF / LEVELS) * ((z0 - z_w[0:48]) + (m0 - tmp3[15:63]))
        drag = jnp.where(bl[...] - 1 == k, 1.0 - DRAG_COEF, 1.0)
        wet = x[WET, k, OWN]
        out_t[k] = wet * (out_t[k] - HEAT_COEF * press)
        out_s[k] = wet * (out_s[k] + SALT_COEF * press)
        out_u[k] = we[k, OWN] * (out_u[k] + z0 * drag - (svt[OWN] + svt[15:63]) + acc[0])
        out_v[k] = wn[k, OWN] * (out_v[k] + m0 * drag + (sut[OWN] + sut[17:65]) + acc[1])
        return press

    lax.fori_loop(0, LEVELS, momentum_level, jnp.zeros((ROWS, LANES), F32))

    for copy in sent:
        copy.wait_send()


def solution(mesh):
    nlon, nlat = mesh.shape["lon"], mesh.shape["lat"]
    inner = next(n for n in (8, 4, 2, 1) if nlat % n == 0 and n * n <= 2 * nlat)
    outer = nlat // inner
    deep = P(None, "lat", "lon")
    flat = P("lat", "lon")

    def step(*args):
        vm = lambda *shape: pltpu.VMEM(shape, F32)
        cube = jax.ShapeDtypeStruct((LEVELS, ROWS, LANES), F32)
        plane = jax.ShapeDtypeStruct((ROWS, LANES), F32)
        level = vm(LEVELS, TALL, LANES)
        copies = 18 + inner - 1 + outer - 1
        scratch = dict(
            x=vm(9, LEVELS, TALL, LANES), lm=pltpu.VMEM((LEVELS, ROWS, LANES), jnp.int32),
            bl=pltpu.VMEM((ROWS, LANES), jnp.int32), stv=vm(ROWS, LANES),
            c1=vm(3, ROWS, LANES), pw1=vm(3, 80, LANES), pe1=vm(3, 80, LANES), m1=vm(3, 80, LANES),
            rn=vm(9, 16, LANES), rs=vm(9, 16, LANES), got_s=vm(9, 16, LANES), got_n=vm(9, 16, LANES),
            tot=vm(8, LANES), slot1=vm(max(inner - 1, 1), 8, LANES), gsum=vm(8, LANES),
            slot2=vm(max(outer - 1, 1), 8, LANES), sfx=vm(96, LANES),
            um0=level, umw=level, vm0=level, we=level, wew=level, wn=level, z1=level, z1w=level,
            mm1=level, mm1e=level, wne=level, tmp3=vm(TALL, LANES), sut=vm(TALL, LANES), svt=vm(TALL, LANES),
            acc=vm(6, ROWS, LANES), acx=vm(8, 64, LANES), c2=vm(2, ROWS, LANES), pw2=vm(2, 80, LANES),
            pe2=vm(2, 80, LANES), m2=vm(2, 80, LANES), sa=vm(11, WIDE, LANES), sb=vm(11, 80, LANES),
            st=vm(3, 2, WIDE, LANES), ou2=vm(2, 2, 80, LANES), cd2=vm(2, 2, 80, LANES), wt2=vm(2, 80, LANES),
            ff2=vm(2, 2, 80, LANES), ga=vm(SUBCYCLES, 2, 2, 80, LANES), gb=vm(SUBCYCLES, 2, 2, 80, LANES),
            fg=vm(2, 2, 80, LANES), tmpb=vm(2, WIDE, LANES), gg=vm(4, 64, LANES),
            in_sem=pltpu.SemaphoreType.DMA((13,)), send_sem=pltpu.SemaphoreType.DMA((copies,)),
            recv_sem=pltpu.SemaphoreType.DMA((copies,)),
        )

        def body(*refs):
            kernel(nlon, nlat, inner, *refs)

        return pl.pallas_call(
            body,
            out_shape=[cube, cube, cube, cube, plane],
            in_specs=[pl.BlockSpec(memory_space=pl.ANY)] * 13,
            out_specs=[pl.BlockSpec(memory_space=pltpu.VMEM)] * 5,
            scratch_shapes=list(scratch.values()),
            compiler_params=pltpu.CompilerParams(
                collective_id=0, has_side_effects=True, vmem_limit_bytes=40 * 1024 * 1024
            ),
        )(*args)

    specs = (deep, deep, deep, deep, flat, deep, flat, deep, deep, deep, deep, flat, flat)
    return jax.shard_map(
        step, mesh=mesh, in_specs=specs, out_specs=(deep, deep, deep, deep, flat), check_vma=False
    )
```

profile of v0, /device:TPU:1, one launch (start us, length us, event | category | flops | bytes accessed | tf_op | source)
XLA Modules:
  0.0 46.6 jit_solution(4206000985119740371)
XLA Ops:
  0.6 0.0 copy-start
  0.6 0.9 %copy-done = f32[8,48,128]{2,1,0:T(8,128)S(1)} copy-done((f32[8,48,128]{2,1,0:T(8,128)S(1)}, f32[8,48,128]{2,1,0:T(8,128)}, u32[]{:S(2)}) %copy-start) | copy-done | bytes 196632
  1.6 0.0 copy-start.1
  1.6 0.9 %copy-done.1 = f32[8,48,128]{2,1,0:T(8,128)S(1)} copy-done((f32[8,48,128]{2,1,0:T(8,128)S(1)}, f32[8,48,128]{2,1,0:T(8,128)}, u32[]{:S(2)}) %copy-start.1) | copy-done | bytes 196632
  2.5 0.0 copy-start.2
  2.5 0.9 %copy-done.2 = f32[8,48,128]{2,1,0:T(8,128)S(1)} copy-done((f32[8,48,128]{2,1,0:T(8,128)S(1)}, f32[8,48,128]{2,1,0:T(8,128)}, u32[]{:S(2)}) %copy-start.2) | copy-done | bytes 196632
  3.4 0.0 copy-start.3
  3.4 0.9 %copy-done.3 = f32[8,48,128]{2,1,0:T(8,128)S(1)} copy-done((f32[8,48,128]{2,1,0:T(8,128)S(1)}, f32[8,48,128]{2,1,0:T(8,128)}, u32[]{:S(2)}) %copy-start.3) | copy-done | bytes 196632
  4.3 0.0 copy-start.4
  4.3 0.9 %copy-done.4 = s32[8,48,128]{2,1,0:T(8,128)S(1)} copy-done((s32[8,48,128]{2,1,0:T(8,128)S(1)}, s32[8,48,128]{2,1,0:T(8,128)}, u32[]{:S(2)}) %copy-start.4) | copy-done | bytes 196632
  5.3 0.0 copy-start.5
  5.3 0.9 %copy-done.5 = f32[8,48,128]{2,1,0:T(8,128)S(1)} copy-done((f32[8,48,128]{2,1,0:T(8,128)S(1)}, f32[8,48,128]{2,1,0:T(8,128)}, u32[]{:S(2)}) %copy-start.5) | copy-done | bytes 196632
  6.2 0.0 copy-start.6
  6.2 0.9 %copy-done.6 = f32[8,48,128]{2,1,0:T(8,128)S(1)} copy-done((f32[8,48,128]{2,1,0:T(8,128)S(1)}, f32[8,48,128]{2,1,0:T(8,128)}, u32[]{:S(2)}) %copy-start.6) | copy-done | bytes 196632
  7.1 0.0 copy-start.7
  7.1 0.9 %copy-done.7 = f32[8,48,128]{2,1,0:T(8,128)S(1)} copy-done((f32[8,48,128]{2,1,0:T(8,128)S(1)}, f32[8,48,128]{2,1,0:T(8,128)}, u32[]{:S(2)}) %copy-start.7) | copy-done | bytes 196632
  8.1 0.0 copy-start.8
  8.1 0.9 %copy-done.8 = f32[8,48,128]{2,1,0:T(8,128)S(1)} copy-done((f32[8,48,128]{2,1,0:T(8,128)S(1)}, f32[8,48,128]{2,1,0:T(8,128)}, u32[]{:S(2)}) %copy-start.8) | copy-done | bytes 196632
  9.0 0.0 copy-start.9
  9.0 0.7 %copy-done.9 = f32[48,128]{1,0:T(8,128)S(1)} copy-done((f32[48,128]{1,0:T(8,128)S(1)}, f32[48,128]{1,0:T(8,128)}, u32[]{:S(2)}) %copy-start.9) | copy-done | bytes 24600
  9.7 0.0 copy-start.10
  9.7 0.7 %copy-done.10 = s32[48,128]{1,0:T(8,128)S(1)} copy-done((s32[48,128]{1,0:T(8,128)S(1)}, s32[48,128]{1,0:T(8,128)}, u32[]{:S(2)}) %copy-start.10) | copy-done | bytes 24600
  10.5 0.0 copy-start.11
  10.5 0.7 %copy-done.11 = f32[48,128]{1,0:T(8,128)S(1)} copy-done((f32[48,128]{1,0:T(8,128)S(1)}, f32[48,128]{1,0:T(8,128)}, u32[]{:S(2)}) %copy-start.11) | copy-done | bytes 24600
  11.2 0.0 copy-start.12
  11.2 0.7 %copy-done.12 = f32[48,128]{1,0:T(8,128)S(1)} copy-done((f32[48,128]{1,0:T(8,128)S(1)}, f32[48,128]{1,0:T(8,128)}, u32[]{:S(2)}) %copy-start.12) | copy-done | bytes 24600
  11.9 31.4 %shard_map.164 = (f32[8,48,128]{2,1,0:T(8,128)S(1)}, f32[8,48,128]{2,1,0:T(8,128)S(1)}, f32[8,48,128]{2,1,0:T(8,128)S(1)}, f32[8,48,128]{2,1,0:T(8,128)S(1)}, f32[48,128]{1,0:T(8,128)S(1)}) custom-call(f32[8,48,128]{2,1,0:T(8,128)S(1)} %copy-done, f32[8,48,128]{2,1,0:T(8,128)S(1)} %copy-done.1, f32[8,48,128]{2,1,0:T(8,128)S(1)} %copy-done.2, ...), custom_call_target="tpu_custom_call" | custom-call | tf_op jit(solution)/shard_map/pallas_call | solution.py:518
  43.3 0.7 %copy.23 = f32[8,48,128]{2,1,0:T(8,128)} copy(f32[8,48,128]{2,1,0:T(8,128)S(1)} %get-tuple-element.10) | data formatting | bytes 393216
  44.0 0.7 %copy.24 = f32[8,48,128]{2,1,0:T(8,128)} copy(f32[8,48,128]{2,1,0:T(8,128)S(1)} %get-tuple-element.11) | data formatting | bytes 393216
  44.7 0.7 %copy.25 = f32[8,48,128]{2,1,0:T(8,128)} copy(f32[8,48,128]{2,1,0:T(8,128)S(1)} %get-tuple-element.12) | data formatting | bytes 393216
  45.4 0.7 %copy.26 = f32[8,48,128]{2,1,0:T(8,128)} copy(f32[8,48,128]{2,1,0:T(8,128)S(1)} %get-tuple-element.13) | data formatting | bytes 393216
  46.0 0.6 %copy.27 = f32[48,128]{1,0:T(8,128)} copy(f32[48,128]{1,0:T(8,128)S(1)} %get-tuple-element.14) | data formatting | bytes 49152
Async XLA Ops:
  0.6 0.9 %copy-start = (f32[8,48,128]{2,1,0:T(8,128)S(1)}, f32[8,48,128]{2,1,0:T(8,128)}, u32[]{:S(2)}) copy-start(f32[8,48,128]{2,1,0:T(8,128)} %refs_0_.1) | copy-start | bytes 589828
  1.6 0.9 %copy-start.1 = (f32[8,48,128]{2,1,0:T(8,128)S(1)}, f32[8,48,128]{2,1,0:T(8,128)}, u32[]{:S(2)}) copy-start(f32[8,48,128]{2,1,0:T(8,128)} %refs_1_.1) | copy-start | bytes 589828
  2.5 0.9 %copy-start.2 = (f32[8,48,128]{2,1,0:T(8,128)S(1)}, f32[8,48,128]{2,1,0:T(8,128)}, u32[]{:S(2)}) copy-start(f32[8,48,128]{2,1,0:T(8,128)} %refs_2_.1) | copy-start | bytes 589828
  3.4 0.9 %copy-start.3 = (f32[8,48,128]{2,1,0:T(8,128)S(1)}, f32[8,48,128]{2,1,0:T(8,128)}, u32[]{:S(2)}) copy-start(f32[8,48,128]{2,1,0:T(8,128)} %refs_3_.1) | copy-start | bytes 589828
  4.3 0.9 %copy-start.4 = (s32[8,48,128]{2,1,0:T(8,128)S(1)}, s32[8,48,128]{2,1,0:T(8,128)}, u32[]{:S(2)}) copy-start(s32[8,48,128]{2,1,0:T(8,128)} %refs_5_.1) | copy-start | bytes 589828
  5.3 0.9 %copy-start.5 = (f32[8,48,128]{2,1,0:T(8,128)S(1)}, f32[8,48,128]{2,1,0:T(8,128)}, u32[]{:S(2)}) copy-start(f32[8,48,128]{2,1,0:T(8,128)} %refs_7_.1) | copy-start | bytes 589828
  6.2 0.9 %copy-start.6 = (f32[8,48,128]{2,1,0:T(8,128)S(1)}, f32[8,48,128]{2,1,0:T(8,128)}, u32[]{:S(2)}) copy-start(f32[8,48,128]{2,1,0:T(8,128)} %refs_8_.1) | copy-start | bytes 589828
  7.1 0.9 %copy-start.7 = (f32[8,48,128]{2,1,0:T(8,128)S(1)}, f32[8,48,128]{2,1,0:T(8,128)}, u32[]{:S(2)}) copy-start(f32[8,48,128]{2,1,0:T(8,128)} %refs_9_.1) | copy-start | bytes 589828
  8.1 0.9 %copy-start.8 = (f32[8,48,128]{2,1,0:T(8,128)S(1)}, f32[8,48,128]{2,1,0:T(8,128)}, u32[]{:S(2)}) copy-start(f32[8,48,128]{2,1,0:T(8,128)} %refs_10_.1) | copy-start | bytes 589828
  9.0 0.7 %copy-start.9 = (f32[48,128]{1,0:T(8,128)S(1)}, f32[48,128]{1,0:T(8,128)}, u32[]{:S(2)}) copy-start(f32[48,128]{1,0:T(8,128)} %refs_4_.1) | copy-start | bytes 73732
  9.7 0.7 %copy-start.10 = (s32[48,128]{1,0:T(8,128)S(1)}, s32[48,128]{1,0:T(8,128)}, u32[]{:S(2)}) copy-start(s32[48,128]{1,0:T(8,128)} %refs_6_.1) | copy-start | bytes 73732
  10.5 0.7 %copy-start.11 = (f32[48,128]{1,0:T(8,128)S(1)}, f32[48,128]{1,0:T(8,128)}, u32[]{:S(2)}) copy-start(f32[48,128]{1,0:T(8,128)} %refs_11_.1) | copy-start | bytes 73732
  11.2 0.7 %copy-start.12 = (f32[48,128]{1,0:T(8,128)S(1)}, f32[48,128]{1,0:T(8,128)}, u32[]{:S(2)}) copy-start(f32[48,128]{1,0:T(8,128)} %refs_12_.1) | copy-start | bytes 73732
where the time goes:
time: 47.2 us; the launch traced here: 46.6 us
  Pallas kernels  31.4 us (67%)
  local copies, waits for them, and re-layouts  14.6 us (31%)
  between operations  0.67 us (1%)
    pallas_call x1, Pallas kernels, step(): pl.pallas_call(body, out_shape=[cube, cube, cube, cube, plane], in_specs=...  31.4 us
    unnamed x31, local copies, waits for them, and re-layouts  14.6 us

commit v1 on v0

--- a/solution.py
+++ b/solution.py
@@ -481,6 +481,15 @@
         copy.wait_send()
 
 
+def store_kernel(*refs):
+    sources, targets, sem = refs[:5], refs[5:10], refs[10]
+    copies = [pltpu.make_async_copy(a, b, sem.at[n]) for n, (a, b) in enumerate(zip(sources, targets))]
+    for copy in copies:
+        copy.start()
+    for copy in copies:
+        copy.wait()
+
+
 def solution(mesh):
     nlon, nlat = mesh.shape["lon"], mesh.shape["lat"]
     inner = next(n for n in (8, 4, 2, 1) if nlat % n == 0 and n * n <= 2 * nlat)
@@ -515,16 +524,23 @@
         def body(*refs):
             kernel(nlon, nlat, inner, *refs)
 
-        return pl.pallas_call(
+        parts = pl.pallas_call(
             body,
             out_shape=[cube, cube, cube, cube, plane],
-            in_specs=[pl.BlockSpec(memory_space=pl.ANY)] * 13,
+            in_specs=[pl.BlockSpec(memory_space=pltpu.HBM)] * 13,
             out_specs=[pl.BlockSpec(memory_space=pltpu.VMEM)] * 5,
             scratch_shapes=list(scratch.values()),
             compiler_params=pltpu.CompilerParams(
                 collective_id=0, has_side_effects=True, vmem_limit_bytes=40 * 1024 * 1024
             ),
-        )(*args)
+        )(*(pltpu.with_memory_space_constraint(a, pltpu.HBM) for a in args))
+        return pl.pallas_call(
+            store_kernel,
+            out_shape=[cube, cube, cube, cube, plane],
+            in_specs=[pl.BlockSpec(memory_space=pltpu.VMEM)] * 5,
+            out_specs=[pl.BlockSpec(memory_space=pltpu.HBM)] * 5,
+            scratch_shapes=[pltpu.SemaphoreType.DMA((5,))],
+        )(*parts)
 
     specs = (deep, deep, deep, deep, flat, deep, flat, deep, deep, deep, deep, flat, flat)
     return jax.shard_map(

time: 47.2 us -> 37.1 us (0.79)
  local copies, waits for them, and re-layouts: 14.6 us -> 3.28 us
  Pallas kernels: 31.4 us -> 33.1 us
    unnamed x31 -> x10, local copies, waits for them, and re-layouts: 14.6 us -> 3.28 us
    pallas_call x0 -> x1, Pallas kernels: none -> 2.13 us  [step(): pl.pallas_call(store_kernel, out_shape=[cube, cube, cube, cube, plane], i...]
where the time goes in v1:
time: 37.1 us; the launch traced here: 37 us
  Pallas kernels  33.1 us (89%)
  local copies, waits for them, and re-layouts  3.28 us (9%)
  between operations  0.66 us (2%)
    pallas_call x1, Pallas kernels, step(): pl.pallas_call(body, out_shape=[cube, cube, cube, cube, plane], in_specs=...  30.9 us
    unnamed x10, local copies, waits for them, and re-layouts  3.28 us
    pallas_call x1, Pallas kernels, step(): pl.pallas_call(store_kernel, out_shape=[cube, cube, cube, cube, plane], i...  2.13 us

profile of v1, /device:TPU:1, one launch (start us, length us, event | category | flops | bytes accessed | tf_op | source)
XLA Modules:
  0.0 37.0 jit_solution(9265715842059620356)
XLA Ops:
  0.6 30.9 %shard_map.164 = (f32[8,48,128]{2,1,0:T(8,128)S(1)}, f32[8,48,128]{2,1,0:T(8,128)S(1)}, f32[8,48,128]{2,1,0:T(8,128)S(1)}, f32[8,48,128]{2,1,0:T(8,128)S(1)}, f32[48,128]{1,0:T(8,128)S(1)}) custom-call(f32[8,48,128]{2,1,0:T(8,128)} %refs_0_.1, f32[8,48,128]{2,1,0:T(8,128)} %refs_1_.1, f32[8,48,128]{2,1,0:T(8,128)} %refs_2_.1, f32[8,48,128]{2,1,0:T(8,128)} %refs_3_.1, ...), custom_call_target="tpu_custom_call" | custom-call | tf_op jit(solution)/shard_map/pallas_call | solution.py:527
  31.6 0.0 copy-start
  31.6 0.7 %copy-done = f32[8,48,128]{2,1,0:T(8,128)} copy-done((f32[8,48,128]{2,1,0:T(8,128)}, f32[8,48,128]{2,1,0:T(8,128)S(1)}, u32[]{:S(2)}) %copy-start) | copy-done | bytes 196632
  32.3 0.0 copy-start.1
  32.3 0.7 %copy-done.1 = f32[8,48,128]{2,1,0:T(8,128)} copy-done((f32[8,48,128]{2,1,0:T(8,128)}, f32[8,48,128]{2,1,0:T(8,128)S(1)}, u32[]{:S(2)}) %copy-start.1) | copy-done | bytes 196632
  32.9 0.0 copy-start.2
  32.9 0.7 %copy-done.2 = f32[8,48,128]{2,1,0:T(8,128)} copy-done((f32[8,48,128]{2,1,0:T(8,128)}, f32[8,48,128]{2,1,0:T(8,128)S(1)}, u32[]{:S(2)}) %copy-start.2) | copy-done | bytes 196632
  33.6 0.0 copy-start.3
  33.6 0.7 %copy-done.3 = f32[8,48,128]{2,1,0:T(8,128)} copy-done((f32[8,48,128]{2,1,0:T(8,128)}, f32[8,48,128]{2,1,0:T(8,128)S(1)}, u32[]{:S(2)}) %copy-start.3) | copy-done | bytes 196632
  34.3 0.0 copy-start.4
  34.3 0.6 %copy-done.4 = f32[48,128]{1,0:T(8,128)} copy-done((f32[48,128]{1,0:T(8,128)}, f32[48,128]{1,0:T(8,128)S(1)}, u32[]{:S(2)}) %copy-start.4) | copy-done | bytes 24600
  34.9 2.1 %shard_map.165 = (f32[8,48,128]{2,1,0:T(8,128)}, f32[8,48,128]{2,1,0:T(8,128)}, f32[8,48,128]{2,1,0:T(8,128)}, f32[8,48,128]{2,1,0:T(8,128)}, f32[48,128]{1,0:T(8,128)}) custom-call(f32[8,48,128]{2,1,0:T(8,128)} %copy-done, f32[8,48,128]{2,1,0:T(8,128)} %copy-done.1, f32[8,48,128]{2,1,0:T(8,128)} %copy-done.2, f32[8,48,128]{2,1,0:T(8,128)} %copy-done.3, ...), custom_call_target="tpu_custom_call" | custom-call | tf_op jit(solution)/shard_map/pallas_call | solution.py:537
Async XLA Ops:
  31.6 0.7 %copy-start = (f32[8,48,128]{2,1,0:T(8,128)}, f32[8,48,128]{2,1,0:T(8,128)S(1)}, u32[]{:S(2)}) copy-start(f32[8,48,128]{2,1,0:T(8,128)S(1)} %get-tuple-element.10.refs_0_) | copy-start | bytes 589828
  32.3 0.7 %copy-start.1 = (f32[8,48,128]{2,1,0:T(8,128)}, f32[8,48,128]{2,1,0:T(8,128)S(1)}, u32[]{:S(2)}) copy-start(f32[8,48,128]{2,1,0:T(8,128)S(1)} %get-tuple-element.11.refs_1_) | copy-start | bytes 589828
  32.9 0.7 %copy-start.2 = (f32[8,48,128]{2,1,0:T(8,128)}, f32[8,48,128]{2,1,0:T(8,128)S(1)}, u32[]{:S(2)}) copy-start(f32[8,48,128]{2,1,0:T(8,128)S(1)} %get-tuple-element.12.refs_2_) | copy-start | bytes 589828
  33.6 0.7 %copy-start.3 = (f32[8,48,128]{2,1,0:T(8,128)}, f32[8,48,128]{2,1,0:T(8,128)S(1)}, u32[]{:S(2)}) copy-start(f32[8,48,128]{2,1,0:T(8,128)S(1)} %get-tuple-element.13.refs_3_) | copy-start | bytes 589828
  34.3 0.6 %copy-start.4 = (f32[48,128]{1,0:T(8,128)}, f32[48,128]{1,0:T(8,128)S(1)}, u32[]{:S(2)}) copy-start(f32[48,128]{1,0:T(8,128)S(1)} %get-tuple-element.14.refs_4_) | copy-start | bytes 73732

commit v2 on v1

--- a/solution.py
+++ b/solution.py
@@ -26,6 +26,7 @@
 THICK_COEF = 0.3
 
 CT, CS, WU, WV, WET, AT, AS, WZ, WM = range(9)
+PACK = ((0, 0), (0, 1), (0, 2), (0, 3), (1, 0), (2, 0), (2, 1), (2, 2), (2, 3))
 OWN = slice(16, 64)
 ZR = slice(16, 72)
 MR = slice(8, 64)
@@ -61,112 +62,160 @@
     nlon, nlat, inner,
     tracer, salinity, zonal, merid, surface, mask, bottom, tr_adj, sa_adj, zo_adj, me_adj, su_adj, st_adj,
     out_t, out_s, out_u, out_v, out_h,
-    x, lm, bl, stv, c1, pw1, pe1, m1, rn, rs, got_s, got_n, tot, slot1, gsum, slot2, sfx,
+    x, lm, bl, stv, c1, ce1, cw1, pw1, pe1, cl, pwl, pel, m1, mr, rn, rs, got_s, got_n,
+    tot, tot_w, tot_e, two, slot1, gsum, slot2, sfx,
     um0, umw, vm0, we, wew, wn, z1, z1w, mm1, mm1e, wne, tmp3, sut, svt,
-    acc, acx, c2, pw2, pe2, m2, sa, sb, st, ou2, cd2, wt2, ff2, ga, gb, fg, tmpb, gg,
+    acc, acx, ce2, cw2, pw2, pe2, m2, sa, sb, st, ou2, cd2, wt2, ff2, ga, gb, fg, tmpb, gg,
     in_sem, send_sem, recv_sem,
 ):
     lon, lat = lax.axis_index("lon"), lax.axis_index("lat")
+    south_here, north_here = lat > 0, lat < nlat - 1
     outer = nlat // inner
+    gi, go = lax.rem(lat, inner), lat // inner
 
     def at(dlon, dlat):
         return (lax.rem(lon + dlon + nlon, nlon), lax.rem(lat + dlat + nlat, nlat))
 
+    def when(condition, action):
+        if condition is None:
+            action()
+        else:
+            pl.when(condition)(action)
+
+    around = [at(*side) for side in SIDES]
+    exists = [{0: None, 1: north_here, -1: south_here}[side[1]] for side in SIDES]
+    from_it = [{0: None, 1: south_here, -1: north_here}[side[1]] for side in SIDES]
+
+    def signal(sem, where, condition):
+        when(condition, lambda: pl.semaphore_signal(sem, inc=1, device_id=where, device_id_type=MESH))
+
+    barrier = pltpu.get_barrier_semaphore()
+    for where, condition in zip(around, exists):
+        signal(barrier, where, condition)
+    mates = [(lon, go * inner + lax.rem(gi + d, inner)) for d in range(1, inner)]
+    peers = [(lon, lax.rem(go + e, outer) * inner + gi) for e in range(1, outer)]
+    for where in mates + peers:
+        signal(barrier, where, None)
+
     loads = []
     for src, dst in (
-        (mask, lm), (bottom, bl), (st_adj, stv),
+        (st_adj, stv), (mask, lm), (bottom, bl),
         (tracer, x.at[CT, :, OWN]), (salinity, x.at[CS, :, OWN]), (zonal, x.at[WU, :, OWN]), (merid, x.at[WV, :, OWN]),
+        (surface, sa.at[SF_H, MINE]), (su_adj, sa.at[SF_HADJ, MINE]),
         (tr_adj, x.at[AT, :, OWN]), (sa_adj, x.at[AS, :, OWN]), (zo_adj, x.at[WZ, :, OWN]), (me_adj, x.at[WM, :, OWN]),
-        (surface, sa.at[SF_H, MINE]), (su_adj, sa.at[SF_HADJ, MINE]),
     ):
         copy = pltpu.make_async_copy(src, dst, in_sem.at[len(loads)])
         copy.start()
         loads.append(copy)
 
-    gi, go = lax.rem(lat, inner), lat // inner
-    mates = [(lon, go * inner + lax.rem(gi + d, inner)) for d in range(1, inner)]
-    peers = [(lon, lax.rem(go + e, outer) * inner + gi) for e in range(1, outer)]
-    around = [at(*side) for side in SIDES]
-
-    barrier = pltpu.get_barrier_semaphore()
-    for where in around + mates + peers:
-        pl.semaphore_signal(barrier, inc=1, device_id=where, device_id_type=MESH)
-
     sent = []
 
-    def send(src, dst, where):
+    def send(src, dst, where, to=None, by=None):
         n = len(sent)
         copy = pltpu.make_async_remote_copy(
             src_ref=src, dst_ref=dst, send_sem=send_sem.at[n], recv_sem=recv_sem.at[n],
             device_id=where, device_id_type=MESH,
         )
-        copy.start()
-        sent.append(copy)
-        return copy
-
-    for copy in loads[:3]:
-        copy.wait()
+        when(to, copy.start)
+        sent.append((copy, to))
+        return copy, by
+
+    def arrive(copies):
+        for copy, by in copies:
+            when(by, copy.wait_recv)
+
     pad = jnp.zeros((8, LANES), F32)
+    loads[0].wait()
     tile_sum = stv[0:8]
     for r in range(1, ROWS // 8):
         tile_sum = tile_sum + stv[8 * r : 8 * r + 8]
     tot[...] = tile_sum
-    pl.semaphore_wait(barrier, len(around) + len(mates) + len(peers))
-    up1 = [send(tot, slot1.at[d - 1], mates[d - 1]) for d in range(1, inner)]
-
-    for copy in loads[3:]:
+    for copy in loads[1:9]:
         copy.wait()
 
     lane = lanes_of(ROWS)
-
-    def mask_level(k, _):
-        bottoms = bl[...]
-        wet = jnp.where((lm[k] > 0) & (k < bottoms), 1.0, 0.0).astype(F32)
-        packs = [c1[0], c1[1], c1[2]]
-        for f in range(9):
-            if f == WET:
-                value = wet
+    EARLY, LATE = (CT, CS, WU, WV, WET), (AT, AS, WZ, WM)
+
+    def mask_fields(fields):
+        def mask_level(k, _):
+            if WET in fields:
+                wet = jnp.where((lm[k] > 0) & (k < bl[...]), 1.0, 0.0).astype(F32)
             else:
-                value = x[f, k, OWN] * wet
-            x[f, k, OWN] = value
-            here = lax.shift_right_logical(lane, 2) == 8 * (f % 4) + k
-            packs[f // 4] = jnp.where(here, roll(value, 32 * (f % 4) + 4 * k + 2), packs[f // 4])
-        for n in range(3):
-            c1[n] = packs[n]
-        return 0
-
-    lax.fori_loop(0, LEVELS, mask_level, 0)
-
-    def pack_rows(f, _):
-        for k in range(LEVELS):
-            rs[f, 2 * k : 2 * k + 2] = x[f, k, 16:18]
-            rn[f, 2 * k : 2 * k + 2] = x[f, k, 62:64]
-        return 0
-
-    lax.fori_loop(0, 9, pack_rows, 0)
+                wet = x[WET, k, OWN]
+            packs = {PACK[f][0]: c1[PACK[f][0]] for f in fields}
+            for f in fields:
+                n, s = PACK[f]
+                value = wet if f == WET else x[f, k, OWN] * wet
+                x[f, k, OWN] = value
+                here = lax.shift_right_logical(lane, 2) == 8 * s + k
+                packs[n] = jnp.where(here, roll(value, 32 * s + 4 * k + 2), packs[n])
+            for n, value in packs.items():
+                c1[n] = value
+            return 0
+
+        lax.fori_loop(0, LEVELS, mask_level, 0)
+
+        def pack_rows(f, _):
+            for k in range(LEVELS):
+                rs[f, 2 * k : 2 * k + 2] = x[f, k, 16:18]
+                rn[f, 2 * k : 2 * k + 2] = x[f, k, 62:64]
+            return 0
+
+        lax.fori_loop(fields[0], fields[-1] + 1, pack_rows, 0)
+
+    c1[1] = jnp.zeros((ROWS, LANES), F32)
+    mask_fields(EARLY)
+    fine, coarse = (lane & 3) < 2, (lane & 31) < 16
+    ce1[...] = jnp.where(fine, c1[0], roll(c1[1], 2))
+    cw1[...] = jnp.where(fine, roll(c1[1], LANES - 2), c1[0])
+    pl.semaphore_wait(barrier, 2 + len(mates) + len(peers) + jnp.where(south_here, 3, 0) + jnp.where(north_here, 3, 0))
+
+    def send_all(table):
+        return [send(src, dst, around[n], exists[n], from_it[n]) for n, src, dst in table]
+
+    def rows_table(first, last):
+        here = slice(first, last)
+        return [(2, rn.at[here], got_s.at[here]), (3, rs.at[here], got_n.at[here])]
+
+    def planes_table(first, last):
+        here = slice(first, last)
+        return [(2, sa.at[here, 56:72], sa.at[here, 8:24]), (3, sa.at[here, 24:40], sa.at[here, 72:88])]
+
+    LOW, HIGH = slice(0, 16), slice(32, 48)
+    phase1 = send_all(
+        [
+            (5, cw1.at[40:48], pe1.at[8:16]),
+            (6, ce1.at[0:8], pw1.at[64:72]),
+            (7, cw1.at[0:8], pe1.at[64:72]),
+            (0, ce1, pw1.at[16:64]),
+            (1, cw1, pe1.at[16:64]),
+        ]
+        + rows_table(0, 5)
+    )
+    level0 = [send(tot, tot_w, around[0]), send(tot, tot_e, around[1])]
+
+    for copy in loads[9:]:
+        copy.wait()
+    mask_fields(LATE)
     sa[SF_WT, MINE] = x[WET, 0, OWN]
-    pack = c1[2]
-    for s, f in ((1, SF_H), (2, SF_HADJ), (3, SF_WT)):
+    pack = roll(sa[SF_H, MINE], 16)
+    for s, f in ((1, SF_HADJ), (2, SF_WT)):
         here = lax.shift_right_logical(lane, 5) == s
-        pack = jnp.where(here, roll(sa[f, MINE], (32 * s + 16) % LANES), pack)
-    c1[2] = pack
-
-    LOW, HIGH = slice(0, 16), slice(32, 48)
-
-    def exchange(c, pw, pe, first, last):
-        return [
-            send(c, pw.at[:, 16:64], around[0]),
-            send(c, pe.at[:, 16:64], around[1]),
-            send(sa.at[first:last, 56:72], sa.at[first:last, 8:24], around[2]),
-            send(sa.at[first:last, 24:40], sa.at[first:last, 72:88], around[3]),
-            send(c.at[:, HIGH], pw.at[:, 0:16], around[4]),
-            send(c.at[:, HIGH], pe.at[:, 0:16], around[5]),
-            send(c.at[:, LOW], pw.at[:, 64:80], around[6]),
-            send(c.at[:, LOW], pe.at[:, 64:80], around[7]),
+        pack = jnp.where(here, roll(sa[f, MINE], 32 * s + 16), pack)
+    cl[0] = c1[2]
+    cl[1] = pack
+    late1 = send_all(
+        rows_table(5, 9)
+        + [
+            (0, cl, pwl.at[:, 16:64]),
+            (1, cl, pel.at[:, 16:64]),
+            (4, cl.at[:, HIGH], pwl.at[:, 0:16]),
+            (5, cl.at[:, HIGH], pel.at[:, 0:16]),
+            (6, cl.at[:, LOW], pwl.at[:, 64:80]),
+            (7, cl.at[:, LOW], pel.at[:, 64:80]),
         ]
-
-    phase1 = [send(rn, got_s, around[2]), send(rs, got_n, around[3])]
-    phase1 += exchange(c1, pw1, pe1, 0, 3)
+        + planes_table(0, 3)
+    )
 
     sfx[0:48] = stv[...]
     for r in range(6):
@@ -184,20 +233,12 @@
     acc[...] = jnp.zeros_like(acc)
     acx[...] = jnp.zeros_like(acx)
 
-    for copy in up1:
-        copy.wait_recv()
-    group = tot[...]
-    above = jnp.zeros((8, LANES), F32)
-    for d in range(1, inner):
-        got = slot1[d - 1]
-        group = group + got
-        above = above + jnp.where(lax.rem(gi - d + inner, inner) > gi, got, 0.0)
-    gsum[...] = group
-    up2 = [send(gsum, slot2.at[e - 1], peers[e - 1]) for e in range(1, outer)]
-
-    for copy in phase1:
-        copy.wait_recv()
-    south_here, north_here = lat > 0, lat < nlat - 1
+    arrive(phase1)
+    arrive(level0)
+    two[0] = tot[...]
+    two[1] = jnp.where(lanes_of(8) < LANES // 2, tot_e[...], tot_w[...])
+    up1 = [send(two, slot1.at[d - 1], mates[d - 1]) for d in range(1, inner)]
+    up1 += send_all([(3, two, slot1.at[inner - 1])])
 
     def unpack_rows(f, _):
         for k in range(LEVELS):
@@ -205,18 +246,20 @@
             x[f, k, 64:66] = jnp.where(north_here, got_n[f, 2 * k : 2 * k + 2], 0.0)
         return 0
 
-    lax.fori_loop(0, 9, unpack_rows, 0)
+    lax.fori_loop(0, 5, unpack_rows, 0)
     lane80 = lanes_of(80)
     rows80 = lax.broadcasted_iota(jnp.int32, (80, LANES), 0)
     inside = ((rows80 >= 16) | south_here) & ((rows80 < 64) | north_here)
     fine = (lane80 & 3) < 2
     coarse = (lane80 & 31) < 16
-    for n in range(3):
-        from_west = fine if n < 2 else jnp.where(lane80 < 32, fine.astype(jnp.int32), coarse.astype(jnp.int32)) > 0
-        m1[n] = jnp.where(inside, jnp.where(from_west, pw1[n], pe1[n]), 0.0)
+
+    rim_w, rim_e = pw1[...], pe1[...]
+    m1[0] = jnp.where(inside, jnp.where(fine, rim_w, rim_e), 0.0)
+    m1[1] = jnp.where(inside, jnp.where(fine, roll(rim_w, LANES - 2), roll(rim_e, 2)), 0.0)
 
     def strip(f, k, rows):
-        return roll(m1[f // 4, rows], 126 - 32 * (f % 4) - 4 * k)
+        n, s = PACK[f]
+        return roll(m1[n, rows], 126 - 32 * s - 4 * k)
 
     def shifted(value, rim, offset):
         ids = lanes_of(value.shape[0])
@@ -247,13 +290,9 @@
         vm0[k, EXT] = v0
         sut[EXT] = u0 + uw
         svt[EXT] = v0 + ve
-        zz = x[WZ, k, EXT] * wet_e
-        mz = x[WM, k, EXT] * wet_n
-        z1[k, EXT] = zz
-        mm1[k, EXT] = mz
-        acx[0] = acx[0] + zz
+        acc[6] = acc[6] + x[WZ, k, OWN] * wet_e[8:56]
+        acc[7] = acc[7] + x[WM, k, OWN] * wet_n[8:56]
         acx[1] = acx[1] + east
-        acx[2] = acx[2] + mz
         acx[3] = acx[3] + north
 
         t0 = SALT_COEF * x[CS, k, OWN] - HEAT_COEF * x[CT, k, OWN]
@@ -279,13 +318,6 @@
     tmp3[72:80] = pad
     lax.fori_loop(0, LEVELS, forward_level, 0)
 
-    for copy in up2:
-        copy.wait_recv()
-    for e in range(1, outer):
-        got = slot2[e - 1]
-        above = above + jnp.where(lax.rem(go - e + outer, outer) > go, got, 0.0)
-    above = jnp.sum(above, axis=0, keepdims=True)
-
     def over(num, count):
         return num / jnp.maximum(count, 1.0)
 
@@ -295,9 +327,10 @@
         acc[0] / LEVELS, acc[1] / LEVELS,
         (acc[2] - acc[0]) / (LEVELS * SUBCYCLES), (acc[3] - acc[1]) / (LEVELS * SUBCYCLES),
         cu, cv,
-        LEVELS * over(acx[0, own], cu) + (sfx[0:48] + above),
-        LEVELS * over(acx[2, own], cv),
+        LEVELS * over(acc[6], cu) + sfx[0:48],
+        LEVELS * over(acc[7], cv),
     ]
+    packs = []
     for n in range(2):
         pack = None
         for s in range(4):
@@ -305,8 +338,25 @@
             sa[SF_U + 4 * n + s, MINE] = value
             turned = roll(value, (32 * s + 16) % LANES)
             pack = turned if s == 0 else jnp.where(lax.shift_right_logical(lane, 5) == s, turned, pack)
-        c2[n] = pack
-    phase2 = exchange(c2, pw2, pe2, 3, 11)
+        packs.append(pack)
+    own_coarse = (lane & 31) < 16
+    ce2[...] = jnp.where(own_coarse, packs[0], roll(packs[1], 16))
+    cw2[...] = jnp.where(own_coarse, roll(packs[1], LANES - 16), packs[0])
+    phase2 = send_all(
+        [
+            (4, ce2.at[HIGH], pw2.at[0:16]),
+            (5, cw2.at[HIGH], pe2.at[0:16]),
+            (6, ce2.at[LOW], pw2.at[64:80]),
+            (7, cw2.at[LOW], pe2.at[64:80]),
+            (0, ce2, pw2.at[16:64]),
+            (1, cw2, pe2.at[16:64]),
+        ]
+        + planes_table(3, 11)
+    )
+    arrive(late1)
+    lax.fori_loop(5, 9, unpack_rows, 0)
+    m1[2] = jnp.where(inside, jnp.where(fine, pwl[0], pel[0]), 0.0)
+    mr[...] = jnp.where(inside, jnp.where(coarse, pwl[1], pel[1]), 0.0)
 
     def advect_level(k, _):
         wet_rim = strip(WET, k, OWN)
@@ -352,22 +402,38 @@
         wne[k, EXT] = north_e
         z1w[k, EXT] = z_w
         mm1e[k, EXT] = m_e
+        zz = x[WZ, k, EXT] * wet_ex
+        mz = x[WM, k, EXT] * x[WET, k, 9:73]
+        z1[k, EXT] = zz
+        mm1[k, EXT] = mz
+        acx[0] = acx[0] + zz
+        acx[2] = acx[2] + mz
         acx[4] = acx[4] + z_w
         acx[5] = acx[5] + east_w
         acx[6] = acx[6] + m_e
         acx[7] = acx[7] + north_e
         return 0
 
-    lax.fori_loop(0, LEVELS, advect_level, 0)
-
-    for copy in phase2:
-        copy.wait_recv()
+    lax.fori_loop(0, LEVELS // 2, advect_level, 0)
+    arrive(up1)
+    group = two[...]
+    above = jnp.zeros((2, 8, LANES), F32)
+    for d in range(1, inner):
+        got = slot1[d - 1]
+        group = group + got
+        above = above + jnp.where(lax.rem(gi - d + inner, inner) > gi, got, 0.0)
+    gsum[...] = group
+    up2 = [send(gsum, slot2.at[e - 1], peers[e - 1]) for e in range(1, outer)]
+    lax.fori_loop(LEVELS // 2, LEVELS, advect_level, 0)
+
+    arrive(phase2)
 
     rim_lane = (lane80 < HALO) | (lane80 >= LANES - HALO)
-    for n in range(2):
-        m2[n] = jnp.where(inside, jnp.where(coarse, pw2[n], pe2[n]), 0.0)
+    rim_w, rim_e = pw2[...], pe2[...]
+    m2[0] = jnp.where(inside, jnp.where(coarse, rim_w, rim_e), 0.0)
+    m2[1] = jnp.where(inside, jnp.where(coarse, roll(rim_w, LANES - 16), roll(rim_e, 16)), 0.0)
     for f in range(11):
-        source, s = (m1[2], f + 1) if f < 3 else (m2[(f - 3) // 4], (f - 3) % 4)
+        source, s = (mr[...], f) if f < 3 else (m2[(f - 3) // 4], (f - 3) % 4)
         sb[f] = jnp.where(rim_lane, roll(source, (LANES - 16 - 32 * s) % LANES), 0.0)
 
     def part(f, p):
@@ -413,9 +479,17 @@
 
     lax.fori_loop(0, SUBCYCLES, sub_step, 0)
 
+    arrive(up2)
+    for e in range(1, outer):
+        got = slot2[e - 1]
+        above = above + jnp.where(lax.rem(go - e + outer, outer) > go, got, 0.0)
     for p in BOTH:
         st[0, p, BODY] = part(SF_HADJ, p)
-        st[1, p, BODY] = part(SF_SU, p)
+        mine = jnp.sum(two[p], axis=0, keepdims=True)
+        north = jnp.sum(jnp.where(north_here, slot1[inner - 1, p], 0.0), axis=0, keepdims=True)
+        beyond = jnp.sum(above[p], axis=0, keepdims=True)
+        suffix = jnp.where(rows80 < 16, beyond + mine, jnp.where(rows80 < 64, beyond, beyond - north))
+        st[1, p, BODY] = part(SF_SU, p) + suffix
         st[2, p, BODY] = part(SF_SV, p)
 
     def back_step(i, _):
@@ -477,8 +551,8 @@
 
     lax.fori_loop(0, LEVELS, momentum_level, jnp.zeros((ROWS, LANES), F32))
 
-    for copy in sent:
-        copy.wait_send()
+    for copy, to in sent:
+        when(to, copy.wait_send)
 
 
 def store_kernel(*refs):
@@ -502,18 +576,19 @@
         cube = jax.ShapeDtypeStruct((LEVELS, ROWS, LANES), F32)
         plane = jax.ShapeDtypeStruct((ROWS, LANES), F32)
         level = vm(LEVELS, TALL, LANES)
-        copies = 18 + inner - 1 + outer - 1
+        copies = 7 + 2 + 10 + inner + 8 + outer - 1
         scratch = dict(
             x=vm(9, LEVELS, TALL, LANES), lm=pltpu.VMEM((LEVELS, ROWS, LANES), jnp.int32),
             bl=pltpu.VMEM((ROWS, LANES), jnp.int32), stv=vm(ROWS, LANES),
-            c1=vm(3, ROWS, LANES), pw1=vm(3, 80, LANES), pe1=vm(3, 80, LANES), m1=vm(3, 80, LANES),
+            c1=vm(3, ROWS, LANES), ce1=vm(ROWS, LANES), cw1=vm(ROWS, LANES), pw1=vm(80, LANES), pe1=vm(80, LANES),
+            cl=vm(2, ROWS, LANES), pwl=vm(2, 80, LANES), pel=vm(2, 80, LANES), m1=vm(3, 80, LANES), mr=vm(80, LANES),
             rn=vm(9, 16, LANES), rs=vm(9, 16, LANES), got_s=vm(9, 16, LANES), got_n=vm(9, 16, LANES),
-            tot=vm(8, LANES), slot1=vm(max(inner - 1, 1), 8, LANES), gsum=vm(8, LANES),
-            slot2=vm(max(outer - 1, 1), 8, LANES), sfx=vm(96, LANES),
+            tot=vm(8, LANES), tot_w=vm(8, LANES), tot_e=vm(8, LANES), two=vm(2, 8, LANES),
+            slot1=vm(inner, 2, 8, LANES), gsum=vm(2, 8, LANES), slot2=vm(max(outer - 1, 1), 2, 8, LANES), sfx=vm(96, LANES),
             um0=level, umw=level, vm0=level, we=level, wew=level, wn=level, z1=level, z1w=level,
             mm1=level, mm1e=level, wne=level, tmp3=vm(TALL, LANES), sut=vm(TALL, LANES), svt=vm(TALL, LANES),
-            acc=vm(6, ROWS, LANES), acx=vm(8, 64, LANES), c2=vm(2, ROWS, LANES), pw2=vm(2, 80, LANES),
-            pe2=vm(2, 80, LANES), m2=vm(2, 80, LANES), sa=vm(11, WIDE, LANES), sb=vm(11, 80, LANES),
+            acc=vm(8, ROWS, LANES), acx=vm(8, 64, LANES), ce2=vm(ROWS, LANES), cw2=vm(ROWS, LANES), pw2=vm(80, LANES),
+            pe2=vm(80, LANES), m2=vm(2, 80, LANES), sa=vm(11, WIDE, LANES), sb=vm(11, 80, LANES),
             st=vm(3, 2, WIDE, LANES), ou2=vm(2, 2, 80, LANES), cd2=vm(2, 2, 80, LANES), wt2=vm(2, 80, LANES),
             ff2=vm(2, 2, 80, LANES), ga=vm(SUBCYCLES, 2, 2, 80, LANES), gb=vm(SUBCYCLES, 2, 2, 80, LANES),
             fg=vm(2, 2, 80, LANES), tmpb=vm(2, WIDE, LANES), gg=vm(4, 64, LANES),
@@ -540,6 +615,7 @@
             in_specs=[pl.BlockSpec(memory_space=pltpu.VMEM)] * 5,
             out_specs=[pl.BlockSpec(memory_space=pltpu.HBM)] * 5,
             scratch_shapes=[pltpu.SemaphoreType.DMA((5,))],
+            compiler_params=pltpu.CompilerParams(vmem_limit_bytes=4 * 1024 * 1024),
         )(*parts)
 
     specs = (deep, deep, deep, deep, flat, deep, flat, deep, deep, deep, deep, flat, flat)

time: 37.1 us -> 29.1 us (0.78)
  Pallas kernels: 33.1 us -> 28.4 us
  local copies, waits for them, and re-layouts: 3.28 us -> 0 us
    pallas_call x1, Pallas kernels: 30.9 us -> 27.5 us  [step(): pl.pallas_call(body, out_shape=[cube, cube, cube, cube, plane], in_specs=...]
    unnamed x10 -> x0, local copies, waits for them, and re-layouts: 3.28 us -> none
    pallas_call x1, Pallas kernels: 2.13 us -> 0.92 us  [step(): pl.pallas_call(store_kernel, out_shape=[cube, cube, cube, cube, plane], i...]
where the time goes in v2:
time: 29.1 us; the launch traced here: 29 us
  Pallas kernels  28.4 us (98%)
  between operations  0.64 us (2%)
    pallas_call x1, Pallas kernels, step(): pl.pallas_call(body, out_shape=[cube, cube, cube, cube, plane], in_specs=...  27.5 us
    pallas_call x1, Pallas kernels, step(): pl.pallas_call(store_kernel, out_shape=[cube, cube, cube, cube, plane], i...  0.92 us

profile of v2, /device:TPU:1, one launch (start us, length us, event | category | flops | bytes accessed | tf_op | source)
XLA Modules:
  0.0 29.0 jit_solution(3719831990928868499)
XLA Ops:
  0.6 27.5 %shard_map.164 = (f32[8,48,128]{2,1,0:T(8,128)S(1)}, f32[8,48,128]{2,1,0:T(8,128)S(1)}, f32[8,48,128]{2,1,0:T(8,128)S(1)}, f32[8,48,128]{2,1,0:T(8,128)S(1)}, f32[48,128]{1,0:T(8,128)S(1)}) custom-call(f32[8,48,128]{2,1,0:T(8,128)} %refs_0_.1, f32[8,48,128]{2,1,0:T(8,128)} %refs_1_.1, f32[8,48,128]{2,1,0:T(8,128)} %refs_2_.1, f32[8,48,128]{2,1,0:T(8,128)} %refs_3_.1, ...), custom_call_target="tpu_custom_call" | custom-call | tf_op jit(solution)/shard_map/pallas_call | solution.py:602
  28.1 0.9 %shard_map.165 = (f32[8,48,128]{2,1,0:T(8,128)}, f32[8,48,128]{2,1,0:T(8,128)}, f32[8,48,128]{2,1,0:T(8,128)}, f32[8,48,128]{2,1,0:T(8,128)}, f32[48,128]{1,0:T(8,128)}) custom-call(f32[8,48,128]{2,1,0:T(8,128)S(1)} %get-tuple-element.10.refs_0_, f32[8,48,128]{2,1,0:T(8,128)S(1)} %get-tuple-element.11.refs_1_, f32[8,48,128]{2,1,0:T(8,128)S(1)} %get-tuple-element.12.refs_2_, ...), custom_call_target="tpu_custom_call" | custom-call | tf_op jit(solution)/shard_map/pallas_call | solution.py:612

commit v3 on v2

--- a/solution.py
+++ b/solution.py
@@ -63,10 +63,10 @@
     tracer, salinity, zonal, merid, surface, mask, bottom, tr_adj, sa_adj, zo_adj, me_adj, su_adj, st_adj,
     out_t, out_s, out_u, out_v, out_h,
     x, lm, bl, stv, c1, ce1, cw1, pw1, pe1, cl, pwl, pel, m1, mr, rn, rs, got_s, got_n,
-    tot, tot_w, tot_e, two, slot1, gsum, slot2, sfx,
+    tot, inn, slot1, gsum, slot2, inn_w, inn_e, sfx,
     um0, umw, vm0, we, wew, wn, z1, z1w, mm1, mm1e, wne, tmp3, sut, svt,
-    acc, acx, ce2, cw2, pw2, pe2, m2, sa, sb, st, ou2, cd2, wt2, ff2, ga, gb, fg, tmpb, gg,
-    in_sem, send_sem, recv_sem,
+    acc, acx, ce2, cw2, pw2, pe2, m2, sa, sb, st, ou2, cd2, wt2, wte, ff2, ga, gb, fg, tmpb, gg,
+    in_sem, send_sem, recv_sem, ready,
 ):
     lon, lat = lax.axis_index("lon"), lax.axis_index("lat")
     south_here, north_here = lat > 0, lat < nlat - 1
@@ -92,10 +92,35 @@
     barrier = pltpu.get_barrier_semaphore()
     for where, condition in zip(around, exists):
         signal(barrier, where, condition)
-    mates = [(lon, go * inner + lax.rem(gi + d, inner)) for d in range(1, inner)]
-    peers = [(lon, lax.rem(go + e, outer) * inner + gi) for e in range(1, outer)]
-    for where in mates + peers:
-        signal(barrier, where, None)
+    chip, even = gi // 2, lax.rem(go, 2) == 0
+    mates = []
+    for d in range(1, inner):
+        there = lax.rem(gi + d, inner)
+        greets = jnp.logical_not(even) | (there // 2 >= chip)
+        greeted = jnp.logical_not(even) | (there // 2 <= chip)
+        mates.append(((lon, go * inner + there), greets, greeted))
+    peers = []
+    for e in range(1, outer):
+        there = lax.rem(go + e, outer)
+        same = lax.rem(there, 2) == lax.rem(go, 2)
+        for c in (0, 1, -1):
+            where = (lax.rem(lon + c + nlon, nlon), there * inner + gi)
+            peers.append((where, same | even, same | jnp.logical_not(even)))
+    greeted_by = 2 + jnp.where(south_here, 3, 0) + jnp.where(north_here, 3, 0)
+    answers = [0, 0]
+    for n, group in enumerate((mates, peers)):
+        for where, greets, greeted in group:
+            signal(barrier, where, greets)
+            greeted_by = greeted_by + jnp.where(greeted, 1, 0)
+            answers[n] = answers[n] + jnp.where(greeted, 0, 1)
+
+    def answer():
+        for n, group in enumerate((mates, peers)):
+            for where, greets, _ in group:
+                signal(ready.at[n], where, jnp.logical_not(greets))
+
+    def wait_answers(n):
+        when(answers[n] > 0, lambda: pl.semaphore_wait(ready.at[n], answers[n]))
 
     loads = []
     for src, dst in (
@@ -116,7 +141,10 @@
             src_ref=src, dst_ref=dst, send_sem=send_sem.at[n], recv_sem=recv_sem.at[n],
             device_id=where, device_id_type=MESH,
         )
-        when(to, copy.start)
+        if to is False:
+            to = None
+        else:
+            when(to, copy.start)
         sent.append((copy, to))
         return copy, by
 
@@ -168,7 +196,7 @@
     fine, coarse = (lane & 3) < 2, (lane & 31) < 16
     ce1[...] = jnp.where(fine, c1[0], roll(c1[1], 2))
     cw1[...] = jnp.where(fine, roll(c1[1], LANES - 2), c1[0])
-    pl.semaphore_wait(barrier, 2 + len(mates) + len(peers) + jnp.where(south_here, 3, 0) + jnp.where(north_here, 3, 0))
+    pl.semaphore_wait(barrier, greeted_by)
 
     def send_all(table):
         return [send(src, dst, around[n], exists[n], from_it[n]) for n, src, dst in table]
@@ -192,7 +220,7 @@
         ]
         + rows_table(0, 5)
     )
-    level0 = [send(tot, tot_w, around[0]), send(tot, tot_e, around[1])]
+    answer()
 
     for copy in loads[9:]:
         copy.wait()
@@ -217,6 +245,9 @@
         + planes_table(0, 3)
     )
 
+    wait_answers(0)
+    up1 = [send(tot, slot1.at[n], mate[0]) for n, mate in enumerate(mates)]
+
     sfx[0:48] = stv[...]
     for r in range(6):
         sfx[48 + 8 * r : 56 + 8 * r] = pad
@@ -228,18 +259,11 @@
             st[n, p, 0:8] = pad
             st[n, p, 88:96] = pad
     for p in range(2):
-        tmpb[p, 0:8] = pad
-        tmpb[p, 88:96] = pad
+        tmpb[p, 8:16] = pad
     acc[...] = jnp.zeros_like(acc)
     acx[...] = jnp.zeros_like(acx)
 
     arrive(phase1)
-    arrive(level0)
-    two[0] = tot[...]
-    two[1] = jnp.where(lanes_of(8) < LANES // 2, tot_e[...], tot_w[...])
-    up1 = [send(two, slot1.at[d - 1], mates[d - 1]) for d in range(1, inner)]
-    up1 += send_all([(3, two, slot1.at[inner - 1])])
-
     def unpack_rows(f, _):
         for k in range(LEVELS):
             x[f, k, 14:16] = jnp.where(south_here, got_s[f, 2 * k : 2 * k + 2], 0.0)
@@ -270,6 +294,25 @@
     row_ids = lax.broadcasted_iota(jnp.int32, (64, LANES), 0) + (lat * ROWS - 8)
     cor = -(1.0 + row_ids.astype(F32) / (ROWS * nlat))
 
+    up2 = [send(inn, inn_w, around[0], False), send(inn, inn_e, around[1], False)]
+    up2 += [send(gsum, slot2.at[n], where, False) for n, (where, _, _) in enumerate(peers)]
+
+    def group_sums():
+        arrive(up1)
+        group = tot[...]
+        above = jnp.zeros((8, LANES), F32)
+        for d in range(1, inner):
+            got = slot1[d - 1]
+            group = group + got
+            above = above + jnp.where(lax.rem(gi - d + inner, inner) > gi, got, 0.0)
+        gsum[...] = group
+        inn[0] = above
+        inn[1] = tot[...]
+        wait_answers(1)
+        for copy, _ in up2:
+            copy.start()
+
+    pl.when(jnp.logical_not(even))(group_sums)
     EXT = slice(8, 72)
 
     def forward_level(k, _):
@@ -316,18 +359,19 @@
         return 0
 
     tmp3[72:80] = pad
-    lax.fori_loop(0, LEVELS, forward_level, 0)
+    lax.fori_loop(0, LEVELS, forward_level, 0, unroll=2)
 
     def over(num, count):
         return num / jnp.maximum(count, 1.0)
 
     own = slice(8, 56)
     cu, cv = acx[1, own], acx[3, own]
+    near = sfx[0:48] - jnp.where(row_ids[0:48] - (lat * ROWS - 8) < ROWS // 2, sfx[0:1], 0.0)
     surf = [
         acc[0] / LEVELS, acc[1] / LEVELS,
         (acc[2] - acc[0]) / (LEVELS * SUBCYCLES), (acc[3] - acc[1]) / (LEVELS * SUBCYCLES),
         cu, cv,
-        LEVELS * over(acc[6], cu) + sfx[0:48],
+        LEVELS * over(acc[6], cu) + near,
         LEVELS * over(acc[7], cv),
     ]
     packs = []
@@ -353,6 +397,7 @@
         ]
         + planes_table(3, 11)
     )
+    pl.when(even)(group_sums)
     arrive(late1)
     lax.fori_loop(5, 9, unpack_rows, 0)
     m1[2] = jnp.where(inside, jnp.where(fine, pwl[0], pel[0]), 0.0)
@@ -414,17 +459,7 @@
         acx[7] = acx[7] + north_e
         return 0
 
-    lax.fori_loop(0, LEVELS // 2, advect_level, 0)
-    arrive(up1)
-    group = two[...]
-    above = jnp.zeros((2, 8, LANES), F32)
-    for d in range(1, inner):
-        got = slot1[d - 1]
-        group = group + got
-        above = above + jnp.where(lax.rem(gi - d + inner, inner) > gi, got, 0.0)
-    gsum[...] = group
-    up2 = [send(gsum, slot2.at[e - 1], peers[e - 1]) for e in range(1, outer)]
-    lax.fori_loop(LEVELS // 2, LEVELS, advect_level, 0)
+    lax.fori_loop(0, LEVELS, advect_level, 0)
 
     arrive(phase2)
 
@@ -453,67 +488,75 @@
             fg[d, p] = jnp.zeros((80, LANES), F32)
 
     BOTH = (0, 1)
-
-    def sub_step(n, _):
-        u = [st[1, p, BODY] for p in BOTH]
-        v = [st[2, p, BODY] for p in BOTH]
-        u_w = pair_west(*u)
-        h = [
-            wt2[p] * (st[0, p, BODY] - DIVERGENCE * ((u[p] - u_w[p]) + (v[p] - st[2, p, 7:87])))
-            for p in BOTH
-        ]
+    wte[0], wte[1] = pair_east(wt2[0], wt2[1])
+
+    def sub_step(n, lo, hi):
+        mid, down, up = slice(lo + 8, hi + 8), slice(lo + 7, hi + 7), slice(lo + 9, hi + 9)
+        rows = slice(lo, hi)
+        u = [st[1, p, mid] for p in BOTH]
+        v = [st[2, p, mid] for p in BOTH]
+        rest = [st[0, p, mid] - DIVERGENCE * (v[p] - st[2, p, down]) - DIVERGENCE * u[p] for p in BOTH]
+        u_w, rest_e = pair_west(*u), pair_east(*rest)
+        h = [wt2[p, rows] * (rest[p] + DIVERGENCE * u_w[p]) for p in BOTH]
+        h_e = [wte[p, rows] * (rest_e[p] + DIVERGENCE * u[p]) for p in BOTH]
         for p in BOTH:
-            st[0, p, BODY] = h[p]
-        h_e = pair_east(*h)
+            st[0, p, mid] = h[p]
         for p in BOTH:
-            for d, old, far in ((0, u[p], h_e[p]), (1, v[p], st[0, p, 9:89])):
+            for d, old, far in ((0, u[p], h_e[p]), (1, v[p], st[0, p, up])):
                 slope = far - h[p]
                 bend = jnp.tanh(0.5 * (h[p] + far))
-                depth = cd2[d, p]
+                depth = cd2[d, p, rows]
                 level = depth * (1.0 + THICK_COEF * bend)
                 tilt = depth * (0.5 * THICK_COEF) * (1.0 - bend * bend) * slope
-                ga[n, d, p] = level - tilt
-                gb[n, d, p] = level + tilt
-                st[1 + d, p, BODY] = (1.0 - FRICTION) * ou2[d, p] * old + ff2[d, p] - level * slope
+                ga[n, d, p, rows] = level - tilt
+                gb[n, d, p, rows] = level + tilt
+                st[1 + d, p, mid] = (1.0 - FRICTION) * ou2[d, p, rows] * old + ff2[d, p, rows] - level * slope
         return 0
 
-    lax.fori_loop(0, SUBCYCLES, sub_step, 0)
+    lax.fori_loop(0, 3, lambda n, _: sub_step(n, 0, 80), 0, unroll=3)
+    lax.fori_loop(3, SUBCYCLES, lambda n, _: sub_step(n, 4, 76), 0, unroll=5)
 
     arrive(up2)
-    for e in range(1, outer):
-        got = slot2[e - 1]
-        above = above + jnp.where(lax.rem(go - e + outer, outer) > go, got, 0.0)
+    sums = []
+    for c, source in enumerate((inn, inn_w, inn_e)):
+        beyond = source[0]
+        for e in range(1, outer):
+            beyond = beyond + jnp.where(lax.rem(go - e + outer, outer) > go, slot2[3 * (e - 1) + c], 0.0)
+        beyond = jnp.sum(beyond, axis=0, keepdims=True)
+        sums.append((beyond, beyond + jnp.sum(source[1], axis=0, keepdims=True)))
+    east_half = lanes_of(1) < LANES // 2
+    sums = (sums[0], tuple(jnp.where(east_half, e, w) for w, e in zip(sums[1], sums[2])))
     for p in BOTH:
         st[0, p, BODY] = part(SF_HADJ, p)
-        mine = jnp.sum(two[p], axis=0, keepdims=True)
-        north = jnp.sum(jnp.where(north_here, slot1[inner - 1, p], 0.0), axis=0, keepdims=True)
-        beyond = jnp.sum(above[p], axis=0, keepdims=True)
-        suffix = jnp.where(rows80 < 16, beyond + mine, jnp.where(rows80 < 64, beyond, beyond - north))
+        suffix = jnp.where(rows80 < HALO + ROWS // 2, sums[p][1], sums[p][0])
         st[1, p, BODY] = part(SF_SU, p) + suffix
         st[2, p, BODY] = part(SF_SV, p)
 
+    mid, down, up, rows = slice(16, 80), slice(15, 79), slice(17, 81), slice(8, 72)
+
     def back_step(i, _):
         n = SUBCYCLES - 1 - i
-        u = [ou2[0, p] * st[1, p, BODY] for p in BOTH]
-        v = [ou2[1, p] * st[2, p, BODY] for p in BOTH]
+        u = [ou2[0, p, rows] * st[1, p, mid] for p in BOTH]
+        v = [ou2[1, p, rows] * st[2, p, mid] for p in BOTH]
         for p in BOTH:
-            fg[0, p] = fg[0, p] + u[p]
-            fg[1, p] = fg[1, p] + v[p]
-            tmpb[p, BODY] = gb[n, 1, p] * v[p]
-        b_w = pair_west(*[gb[n, 0, p] * u[p] for p in BOTH])
-        h = [
-            wt2[p] * (st[0, p, BODY] + (ga[n, 0, p] * u[p] - b_w[p]) + (ga[n, 1, p] * v[p] - tmpb[p, 7:87]))
-            for p in BOTH
+            fg[0, p, rows] = fg[0, p, rows] + u[p]
+            fg[1, p, rows] = fg[1, p, rows] + v[p]
+            tmpb[p, mid] = gb[n, 1, p, rows] * v[p]
+        b_u = [gb[n, 0, p, rows] * u[p] for p in BOTH]
+        rest = [
+            st[0, p, mid] + ga[n, 0, p, rows] * u[p] + (ga[n, 1, p, rows] * v[p] - tmpb[p, down]) for p in BOTH
         ]
+        b_w, rest_e = pair_west(*b_u), pair_east(*rest)
+        h = [wt2[p, rows] * (rest[p] - b_w[p]) for p in BOTH]
+        h_e = [wte[p, rows] * (rest_e[p] - b_u[p]) for p in BOTH]
         for p in BOTH:
-            st[0, p, BODY] = h[p]
-        h_e = pair_east(*h)
+            st[0, p, mid] = h[p]
         for p in BOTH:
-            st[1, p, BODY] = (1.0 - FRICTION) * u[p] - DIVERGENCE * (h[p] - h_e[p])
-            st[2, p, BODY] = (1.0 - FRICTION) * v[p] - DIVERGENCE * (h[p] - st[0, p, 9:89])
+            st[1, p, mid] = (1.0 - FRICTION) * u[p] - DIVERGENCE * (h[p] - h_e[p])
+            st[2, p, mid] = (1.0 - FRICTION) * v[p] - DIVERGENCE * (h[p] - st[0, p, up])
         return 0
 
-    lax.fori_loop(0, SUBCYCLES, back_step, 0)
+    lax.fori_loop(0, SUBCYCLES, back_step, 0, unroll=8)
 
     out_h[...] = st[0, 0, MINE]
     window = slice(8, 72)
@@ -576,24 +619,25 @@
         cube = jax.ShapeDtypeStruct((LEVELS, ROWS, LANES), F32)
         plane = jax.ShapeDtypeStruct((ROWS, LANES), F32)
         level = vm(LEVELS, TALL, LANES)
-        copies = 7 + 2 + 10 + inner + 8 + outer - 1
+        copies = 7 + 10 + inner - 1 + 8 + 2 + 3 * (outer - 1)
         scratch = dict(
             x=vm(9, LEVELS, TALL, LANES), lm=pltpu.VMEM((LEVELS, ROWS, LANES), jnp.int32),
             bl=pltpu.VMEM((ROWS, LANES), jnp.int32), stv=vm(ROWS, LANES),
             c1=vm(3, ROWS, LANES), ce1=vm(ROWS, LANES), cw1=vm(ROWS, LANES), pw1=vm(80, LANES), pe1=vm(80, LANES),
             cl=vm(2, ROWS, LANES), pwl=vm(2, 80, LANES), pel=vm(2, 80, LANES), m1=vm(3, 80, LANES), mr=vm(80, LANES),
             rn=vm(9, 16, LANES), rs=vm(9, 16, LANES), got_s=vm(9, 16, LANES), got_n=vm(9, 16, LANES),
-            tot=vm(8, LANES), tot_w=vm(8, LANES), tot_e=vm(8, LANES), two=vm(2, 8, LANES),
-            slot1=vm(inner, 2, 8, LANES), gsum=vm(2, 8, LANES), slot2=vm(max(outer - 1, 1), 2, 8, LANES), sfx=vm(96, LANES),
+            tot=vm(8, LANES), inn=vm(2, 8, LANES), slot1=vm(max(inner - 1, 1), 8, LANES), gsum=vm(8, LANES),
+            slot2=vm(max(3 * (outer - 1), 1), 8, LANES), inn_w=vm(2, 8, LANES), inn_e=vm(2, 8, LANES), sfx=vm(96, LANES),
             um0=level, umw=level, vm0=level, we=level, wew=level, wn=level, z1=level, z1w=level,
             mm1=level, mm1e=level, wne=level, tmp3=vm(TALL, LANES), sut=vm(TALL, LANES), svt=vm(TALL, LANES),
             acc=vm(8, ROWS, LANES), acx=vm(8, 64, LANES), ce2=vm(ROWS, LANES), cw2=vm(ROWS, LANES), pw2=vm(80, LANES),
             pe2=vm(80, LANES), m2=vm(2, 80, LANES), sa=vm(11, WIDE, LANES), sb=vm(11, 80, LANES),
-            st=vm(3, 2, WIDE, LANES), ou2=vm(2, 2, 80, LANES), cd2=vm(2, 2, 80, LANES), wt2=vm(2, 80, LANES),
+            st=vm(3, 2, WIDE, LANES), ou2=vm(2, 2, 80, LANES), cd2=vm(2, 2, 80, LANES), wt2=vm(2, 80, LANES), wte=vm(2, 80, LANES),
             ff2=vm(2, 2, 80, LANES), ga=vm(SUBCYCLES, 2, 2, 80, LANES), gb=vm(SUBCYCLES, 2, 2, 80, LANES),
             fg=vm(2, 2, 80, LANES), tmpb=vm(2, WIDE, LANES), gg=vm(4, 64, LANES),
             in_sem=pltpu.SemaphoreType.DMA((13,)), send_sem=pltpu.SemaphoreType.DMA((copies,)),
             recv_sem=pltpu.SemaphoreType.DMA((copies,)),
+            ready=pltpu.SemaphoreType.REGULAR((2,)),
         )
 
         def body(*refs):

time: 29.1 us -> 27 us (0.928)
  the two profiles are of different devices: /device:TPU:1 before, /device:TPU:2 now
where the time goes in v3:
time: 27 us; the launch traced here: 26.9 us
  Pallas kernels  26.3 us (97%)
  between operations  0.64 us (2%)
    pallas_call x1, Pallas kernels, step(): pl.pallas_call(body, out_shape=[cube, cube, cube, cube, plane], in_specs=...  25.3 us
    pallas_call x1, Pallas kernels, step(): pl.pallas_call(store_kernel, out_shape=[cube, cube, cube, cube, plane], i...  0.92 us

profile of v3, /device:TPU:2, one launch (start us, length us, event | category | flops | bytes accessed | tf_op | source)
XLA Modules:
  0.0 26.9 jit_solution(6387877479553718702)
XLA Ops:
  0.6 25.3 %shard_map.164 = (f32[8,48,128]{2,1,0:T(8,128)S(1)}, f32[8,48,128]{2,1,0:T(8,128)S(1)}, f32[8,48,128]{2,1,0:T(8,128)S(1)}, f32[8,48,128]{2,1,0:T(8,128)S(1)}, f32[48,128]{1,0:T(8,128)S(1)}) custom-call(f32[8,48,128]{2,1,0:T(8,128)} %refs_0_.1, f32[8,48,128]{2,1,0:T(8,128)} %refs_1_.1, f32[8,48,128]{2,1,0:T(8,128)} %refs_2_.1, f32[8,48,128]{2,1,0:T(8,128)} %refs_3_.1, ...), custom_call_target="tpu_custom_call" | custom-call | tf_op jit(solution)/shard_map/pallas_call | solution.py:646
  26.0 0.9 %shard_map.165 = (f32[8,48,128]{2,1,0:T(8,128)}, f32[8,48,128]{2,1,0:T(8,128)}, f32[8,48,128]{2,1,0:T(8,128)}, f32[8,48,128]{2,1,0:T(8,128)}, f32[48,128]{1,0:T(8,128)}) custom-call(f32[8,48,128]{2,1,0:T(8,128)S(1)} %get-tuple-element.10.refs_0_, f32[8,48,128]{2,1,0:T(8,128)S(1)} %get-tuple-element.11.refs_1_, f32[8,48,128]{2,1,0:T(8,128)S(1)} %get-tuple-element.12.refs_2_, ...), custom_call_target="tpu_custom_call" | custom-call | tf_op jit(solution)/shard_map/pallas_call | solution.py:656

commit v4 on v3

--- a/solution.py
+++ b/solution.py
@@ -102,22 +102,28 @@
     peers = []
     for e in range(1, outer):
         there = lax.rem(go + e, outer)
-        same = lax.rem(there, 2) == lax.rem(go, 2)
-        for c in (0, 1, -1):
-            where = (lax.rem(lon + c + nlon, nlon), there * inner + gi)
-            peers.append((where, same | even, same | jnp.logical_not(even)))
+        down = go > there
+        facing = jnp.where(lax.rem(there + go, 2) == 0, gi, inner - 1 - gi)
+        hasty = jnp.where(down, go, there) % 2 < jnp.where(down, there, go) % 2
+        for c in (1, -1, 0):
+            where = (lax.rem(lon + c + nlon, nlon), there * inner + facing)
+            peers.append((where, down == hasty, down != hasty, down, hasty))
     greeted_by = 2 + jnp.where(south_here, 3, 0) + jnp.where(north_here, 3, 0)
     answers = [0, 0]
-    for n, group in enumerate((mates, peers)):
-        for where, greets, greeted in group:
-            signal(barrier, where, greets)
-            greeted_by = greeted_by + jnp.where(greeted, 1, 0)
-            answers[n] = answers[n] + jnp.where(greeted, 0, 1)
+    for where, greets, greeted in mates:
+        signal(barrier, where, greets)
+        greeted_by = greeted_by + jnp.where(greeted, 1, 0)
+        answers[0] = answers[0] + jnp.where(greeted, 0, 1)
+    for where, greets, greeted, down, hasty in peers:
+        signal(barrier, where, greets)
+        greeted_by = greeted_by + jnp.where(greeted, 1, 0)
+        answers[1] = answers[1] + jnp.where(down & hasty, 1, 0)
 
     def answer():
-        for n, group in enumerate((mates, peers)):
-            for where, greets, _ in group:
-                signal(ready.at[n], where, jnp.logical_not(greets))
+        for where, greets, _ in mates:
+            signal(ready.at[0], where, jnp.logical_not(greets))
+        for where, _, _, down, hasty in peers:
+            signal(ready.at[1], where, hasty & jnp.logical_not(down))
 
     def wait_answers(n):
         when(answers[n] > 0, lambda: pl.semaphore_wait(ready.at[n], answers[n]))
@@ -135,16 +141,14 @@
 
     sent = []
 
-    def send(src, dst, where, to=None, by=None):
+    def send(src, dst, where, to=None, by=None, now=None):
         n = len(sent)
         copy = pltpu.make_async_remote_copy(
             src_ref=src, dst_ref=dst, send_sem=send_sem.at[n], recv_sem=recv_sem.at[n],
             device_id=where, device_id_type=MESH,
         )
-        if to is False:
-            to = None
-        else:
-            when(to, copy.start)
+        if now is not False:
+            when(to if now is None else now, copy.start)
         sent.append((copy, to))
         return copy, by
 
@@ -181,7 +185,7 @@
                 c1[n] = value
             return 0
 
-        lax.fori_loop(0, LEVELS, mask_level, 0)
+        lax.fori_loop(0, LEVELS, mask_level, 0, unroll=4)
 
         def pack_rows(f, _):
             for k in range(LEVELS):
@@ -220,6 +224,14 @@
         ]
         + rows_table(0, 5)
     )
+    up1 = [send(tot, slot1.at[n], mate[0], now=False) for n, mate in enumerate(mates)]
+
+    def member_sums():
+        wait_answers(0)
+        for copy, _ in up1:
+            copy.start()
+
+    pl.when(jnp.logical_not(even))(member_sums)
     answer()
 
     for copy in loads[9:]:
@@ -245,8 +257,7 @@
         + planes_table(0, 3)
     )
 
-    wait_answers(0)
-    up1 = [send(tot, slot1.at[n], mate[0]) for n, mate in enumerate(mates)]
+    pl.when(even)(member_sums)
 
     sfx[0:48] = stv[...]
     for r in range(6):
@@ -263,39 +274,10 @@
     acc[...] = jnp.zeros_like(acc)
     acx[...] = jnp.zeros_like(acx)
 
-    arrive(phase1)
-    def unpack_rows(f, _):
-        for k in range(LEVELS):
-            x[f, k, 14:16] = jnp.where(south_here, got_s[f, 2 * k : 2 * k + 2], 0.0)
-            x[f, k, 64:66] = jnp.where(north_here, got_n[f, 2 * k : 2 * k + 2], 0.0)
-        return 0
-
-    lax.fori_loop(0, 5, unpack_rows, 0)
-    lane80 = lanes_of(80)
-    rows80 = lax.broadcasted_iota(jnp.int32, (80, LANES), 0)
-    inside = ((rows80 >= 16) | south_here) & ((rows80 < 64) | north_here)
-    fine = (lane80 & 3) < 2
-    coarse = (lane80 & 31) < 16
-
-    rim_w, rim_e = pw1[...], pe1[...]
-    m1[0] = jnp.where(inside, jnp.where(fine, rim_w, rim_e), 0.0)
-    m1[1] = jnp.where(inside, jnp.where(fine, roll(rim_w, LANES - 2), roll(rim_e, 2)), 0.0)
-
-    def strip(f, k, rows):
-        n, s = PACK[f]
-        return roll(m1[n, rows], 126 - 32 * s - 4 * k)
-
-    def shifted(value, rim, offset):
-        ids = lanes_of(value.shape[0])
-        if offset > 0:
-            return roll(jnp.where(ids < offset, rim, value), LANES - offset)
-        return roll(jnp.where(ids >= LANES + offset, rim, value), -offset)
-
-    row_ids = lax.broadcasted_iota(jnp.int32, (64, LANES), 0) + (lat * ROWS - 8)
-    cor = -(1.0 + row_ids.astype(F32) / (ROWS * nlat))
-
-    up2 = [send(inn, inn_w, around[0], False), send(inn, inn_e, around[1], False)]
-    up2 += [send(gsum, slot2.at[n], where, False) for n, (where, _, _) in enumerate(peers)]
+    up2 = [send(inn, inn_w, around[0], now=False), send(inn, inn_e, around[1], now=False)]
+    for n, (where, _, _, down, hasty) in enumerate(peers):
+        come = lax.rem(go - n // 3 - 1 + outer, outer) > go
+        up2.append(send(gsum, slot2.at[n], where, down, come, False))
 
     def group_sums():
         arrive(up1)
@@ -308,11 +290,43 @@
         gsum[...] = group
         inn[0] = above
         inn[1] = tot[...]
-        wait_answers(1)
-        for copy, _ in up2:
+        for copy, _ in up2[:2]:
             copy.start()
+        for (copy, _), (_, _, _, down, hasty) in zip(up2[2:], peers):
+            when(down & jnp.logical_not(hasty), copy.start)
 
     pl.when(jnp.logical_not(even))(group_sums)
+    arrive(phase1)
+    def unpack_rows(f, _):
+        for k in range(LEVELS):
+            x[f, k, 14:16] = jnp.where(south_here, got_s[f, 2 * k : 2 * k + 2], 0.0)
+            x[f, k, 64:66] = jnp.where(north_here, got_n[f, 2 * k : 2 * k + 2], 0.0)
+        return 0
+
+    lax.fori_loop(0, 5, unpack_rows, 0)
+    lane80 = lanes_of(80)
+    rows80 = lax.broadcasted_iota(jnp.int32, (80, LANES), 0)
+    inside = ((rows80 >= 16) | south_here) & ((rows80 < 64) | north_here)
+    fine = (lane80 & 3) < 2
+    coarse = (lane80 & 31) < 16
+
+    rim_w, rim_e = pw1[...], pe1[...]
+    m1[0] = jnp.where(inside, jnp.where(fine, rim_w, rim_e), 0.0)
+    m1[1] = jnp.where(inside, jnp.where(fine, roll(rim_w, LANES - 2), roll(rim_e, 2)), 0.0)
+
+    def strip(f, k, rows):
+        n, s = PACK[f]
+        return roll(m1[n, rows], 126 - 32 * s - 4 * k)
+
+    def shifted(value, rim, offset):
+        ids = lanes_of(value.shape[0])
+        if offset > 0:
+            return roll(jnp.where(ids < offset, rim, value), LANES - offset)
+        return roll(jnp.where(ids >= LANES + offset, rim, value), -offset)
+
+    row_ids = lax.broadcasted_iota(jnp.int32, (64, LANES), 0) + (lat * ROWS - 8)
+    cor = -(1.0 + row_ids.astype(F32) / (ROWS * nlat))
+
     EXT = slice(8, 72)
 
     def forward_level(k, _):
@@ -398,6 +412,9 @@
         + planes_table(3, 11)
     )
     pl.when(even)(group_sums)
+    wait_answers(1)
+    for copy, (_, _, _, down, hasty) in zip(up2[2:], peers):
+        when(down & hasty, copy[0].start)
     arrive(late1)
     lax.fori_loop(5, 9, unpack_rows, 0)
     m1[2] = jnp.where(inside, jnp.where(fine, pwl[0], pel[0]), 0.0)
@@ -518,14 +535,14 @@
 
     arrive(up2)
     sums = []
-    for c, source in enumerate((inn, inn_w, inn_e)):
+    for c, source in enumerate((inn_w, inn_e, inn)):
         beyond = source[0]
         for e in range(1, outer):
             beyond = beyond + jnp.where(lax.rem(go - e + outer, outer) > go, slot2[3 * (e - 1) + c], 0.0)
         beyond = jnp.sum(beyond, axis=0, keepdims=True)
         sums.append((beyond, beyond + jnp.sum(source[1], axis=0, keepdims=True)))
     east_half = lanes_of(1) < LANES // 2
-    sums = (sums[0], tuple(jnp.where(east_half, e, w) for w, e in zip(sums[1], sums[2])))
+    sums = (sums[2], tuple(jnp.where(east_half, e, w) for w, e in zip(sums[0], sums[1])))
     for p in BOTH:
         st[0, p, BODY] = part(SF_HADJ, p)
         suffix = jnp.where(rows80 < HALO + ROWS // 2, sums[p][1], sums[p][0])

time: 27 us -> 25.7 us (0.952)
  the two profiles are of different devices: /device:TPU:2 before, /device:TPU:97 now
where the time goes in v4:
time: 25.7 us; the launch traced here: 25.6 us
  Pallas kernels  24.9 us (97%)
  between operations  0.64 us (2%)
    pallas_call x1, Pallas kernels, step(): pl.pallas_call(body, out_shape=[cube, cube, cube, cube, plane], in_specs=...  24 us
    pallas_call x1, Pallas kernels, step(): pl.pallas_call(store_kernel, out_shape=[cube, cube, cube, cube, plane], i...  0.92 us

profile of v4, /device:TPU:97, one launch (start us, length us, event | category | flops | bytes accessed | tf_op | source)
XLA Modules:
  0.0 25.6 jit_solution(9127614491895973888)
XLA Ops:
  0.6 24.0 %shard_map.164 = (f32[8,48,128]{2,1,0:T(8,128)S(1)}, f32[8,48,128]{2,1,0:T(8,128)S(1)}, f32[8,48,128]{2,1,0:T(8,128)S(1)}, f32[8,48,128]{2,1,0:T(8,128)S(1)}, f32[48,128]{1,0:T(8,128)S(1)}) custom-call(f32[8,48,128]{2,1,0:T(8,128)} %refs_0_.1, f32[8,48,128]{2,1,0:T(8,128)} %refs_1_.1, f32[8,48,128]{2,1,0:T(8,128)} %refs_2_.1, f32[8,48,128]{2,1,0:T(8,128)} %refs_3_.1, ...), custom_call_target="tpu_custom_call" | custom-call | tf_op jit(solution)/shard_map/pallas_call | solution.py:663
  24.7 0.9 %shard_map.165 = (f32[8,48,128]{2,1,0:T(8,128)}, f32[8,48,128]{2,1,0:T(8,128)}, f32[8,48,128]{2,1,0:T(8,128)}, f32[8,48,128]{2,1,0:T(8,128)}, f32[48,128]{1,0:T(8,128)}) custom-call(f32[8,48,128]{2,1,0:T(8,128)S(1)} %get-tuple-element.10.refs_0_, f32[8,48,128]{2,1,0:T(8,128)S(1)} %get-tuple-element.11.refs_1_, f32[8,48,128]{2,1,0:T(8,128)S(1)} %get-tuple-element.12.refs_2_, ...), custom_call_target="tpu_custom_call" | custom-call | tf_op jit(solution)/shard_map/pallas_call | solution.py:673

commit v5 on v4

--- a/solution.py
+++ b/solution.py
@@ -327,6 +327,8 @@
     row_ids = lax.broadcasted_iota(jnp.int32, (64, LANES), 0) + (lat * ROWS - 8)
     cor = -(1.0 + row_ids.astype(F32) / (ROWS * nlat))
 
+    m2[0] = SALT_COEF * roll(m1[0], LANES - 32) - HEAT_COEF * m1[0]
+
     EXT = slice(8, 72)
 
     def forward_level(k, _):
@@ -340,13 +342,13 @@
         wu, wv = x[WU, k, EXT], x[WV, k, EXT]
         u0 = wu * wet_e
         v0 = wv * wet_n
-        uw = shifted(wu, strip(WU, k, EXT), -1) * wet
-        ve = shifted(wv, strip(WV, k, EXT), 1) * tmp3[9:73]
+        uw = shifted(wu[8:64], strip(WU, k, ZR), -1) * wet[8:64]
+        ve = shifted(wv[0:56], strip(WV, k, MR), 1) * tmp3[9:65]
         um0[k, EXT] = u0
-        umw[k, EXT] = uw
+        umw[k, ZR] = uw
         vm0[k, EXT] = v0
-        sut[EXT] = u0 + uw
-        svt[EXT] = v0 + ve
+        sut[ZR] = u0[8:64] + uw
+        svt[MR] = v0[0:56] + ve
         acc[6] = acc[6] + x[WZ, k, OWN] * wet_e[8:56]
         acc[7] = acc[7] + x[WM, k, OWN] * wet_n[8:56]
         acx[1] = acx[1] + east
@@ -354,7 +356,7 @@
 
         t0 = SALT_COEF * x[CS, k, OWN] - HEAT_COEF * x[CT, k, OWN]
         tn = SALT_COEF * x[CS, k, 17:65] - HEAT_COEF * x[CT, k, 17:65]
-        te = shifted(t0, SALT_COEF * strip(CS, k, OWN) - HEAT_COEF * strip(CT, k, OWN), 1)
+        te = shifted(t0, roll(m2[0, OWN], 126 - 4 * k), 1)
         dpe = acc[4] + (te - t0)
         dpn = acc[5] + (tn - t0)
         acc[4] = dpe
@@ -478,6 +480,8 @@
 
     lax.fori_loop(0, LEVELS, advect_level, 0)
 
+    for copy, to in sent:
+        when(to, copy.wait_send)
     arrive(phase2)
 
     rim_lane = (lane80 < HALO) | (lane80 >= LANES - HALO)
@@ -610,9 +614,6 @@
         return press
 
     lax.fori_loop(0, LEVELS, momentum_level, jnp.zeros((ROWS, LANES), F32))
-
-    for copy, to in sent:
-        when(to, copy.wait_send)
 
 
 def store_kernel(*refs):

time: 25.7 us -> 25.5 us (level)
  the two profiles are of different devices: /device:TPU:97 before, /device:TPU:1 now
where the time goes in v5:
time: 25.5 us; the launch traced here: 25.1 us
  Pallas kernels  24.5 us (96%)
  between operations  0.64 us (3%)
    pallas_call x1, Pallas kernels, step(): pl.pallas_call(body, out_shape=[cube, cube, cube, cube, plane], in_specs=...  23.6 us
    pallas_call x1, Pallas kernels, step(): pl.pallas_call(store_kernel, out_shape=[cube, cube, cube, cube, plane], i...  0.92 us

profile of v5, /device:TPU:1, one launch (start us, length us, event | category | flops | bytes accessed | tf_op | source)
XLA Modules:
  0.0 25.1 jit_solution(5219940191469145051)
XLA Ops:
  0.6 23.6 %shard_map.164 = (f32[8,48,128]{2,1,0:T(8,128)S(1)}, f32[8,48,128]{2,1,0:T(8,128)S(1)}, f32[8,48,128]{2,1,0:T(8,128)S(1)}, f32[8,48,128]{2,1,0:T(8,128)S(1)}, f32[48,128]{1,0:T(8,128)S(1)}) custom-call(f32[8,48,128]{2,1,0:T(8,128)} %refs_0_.1, f32[8,48,128]{2,1,0:T(8,128)} %refs_1_.1, f32[8,48,128]{2,1,0:T(8,128)} %refs_2_.1, f32[8,48,128]{2,1,0:T(8,128)} %refs_3_.1, ...), custom_call_target="tpu_custom_call" | custom-call | tf_op jit(solution)/shard_map/pallas_call | solution.py:664
  24.2 0.9 %shard_map.165 = (f32[8,48,128]{2,1,0:T(8,128)}, f32[8,48,128]{2,1,0:T(8,128)}, f32[8,48,128]{2,1,0:T(8,128)}, f32[8,48,128]{2,1,0:T(8,128)}, f32[48,128]{1,0:T(8,128)}) custom-call(f32[8,48,128]{2,1,0:T(8,128)S(1)} %get-tuple-element.10.refs_0_, f32[8,48,128]{2,1,0:T(8,128)S(1)} %get-tuple-element.11.refs_1_, f32[8,48,128]{2,1,0:T(8,128)S(1)} %get-tuple-element.12.refs_2_, ...), custom_call_target="tpu_custom_call" | custom-call | tf_op jit(solution)/shard_map/pallas_call | solution.py:674

commit v6 on v5

--- a/solution.py
+++ b/solution.py
@@ -553,9 +553,8 @@
         st[1, p, BODY] = part(SF_SU, p) + suffix
         st[2, p, BODY] = part(SF_SV, p)
 
-    mid, down, up, rows = slice(16, 80), slice(15, 79), slice(17, 81), slice(8, 72)
-
-    def back_step(i, _):
+    def back_step(i, lo, hi):
+        mid, down, up, rows = slice(lo + 8, hi + 8), slice(lo + 7, hi + 7), slice(lo + 9, hi + 9), slice(lo, hi)
         n = SUBCYCLES - 1 - i
         u = [ou2[0, p, rows] * st[1, p, mid] for p in BOTH]
         v = [ou2[1, p, rows] * st[2, p, mid] for p in BOTH]
@@ -577,7 +576,8 @@
             st[2, p, mid] = (1.0 - FRICTION) * v[p] - DIVERGENCE * (h[p] - st[0, p, up])
         return 0
 
-    lax.fori_loop(0, SUBCYCLES, back_step, 0, unroll=8)
+    lax.fori_loop(0, 4, lambda i, _: back_step(i, 8, 72), 0, unroll=4)
+    lax.fori_loop(4, SUBCYCLES, lambda i, _: back_step(i, 12, 68), 0, unroll=4)
 
     out_h[...] = st[0, 0, MINE]
     window = slice(8, 72)

time: 25.5 us -> 25.5 us (level)
  no operation moved by 1% of the time
where the time goes in v6:
time: 25.5 us; the launch traced here: 25.1 us
  Pallas kernels  24.5 us (96%)
  between operations  0.64 us (3%)
    pallas_call x1, Pallas kernels, step(): pl.pallas_call(body, out_shape=[cube, cube, cube, cube, plane], in_specs=...  23.6 us
    pallas_call x1, Pallas kernels, step(): pl.pallas_call(store_kernel, out_shape=[cube, cube, cube, cube, plane], i...  0.92 us

profile of v6, /device:TPU:1, one launch (start us, length us, event | category | flops | bytes accessed | tf_op | source)
XLA Modules:
  0.0 25.1 jit_solution(6291607054027522845)
XLA Ops:
  0.6 23.6 %shard_map.164 = (f32[8,48,128]{2,1,0:T(8,128)S(1)}, f32[8,48,128]{2,1,0:T(8,128)S(1)}, f32[8,48,128]{2,1,0:T(8,128)S(1)}, f32[8,48,128]{2,1,0:T(8,128)S(1)}, f32[48,128]{1,0:T(8,128)S(1)}) custom-call(f32[8,48,128]{2,1,0:T(8,128)} %refs_0_.1, f32[8,48,128]{2,1,0:T(8,128)} %refs_1_.1, f32[8,48,128]{2,1,0:T(8,128)} %refs_2_.1, f32[8,48,128]{2,1,0:T(8,128)} %refs_3_.1, ...), custom_call_target="tpu_custom_call" | custom-call | tf_op jit(solution)/shard_map/pallas_call | solution.py:664
  24.2 0.9 %shard_map.165 = (f32[8,48,128]{2,1,0:T(8,128)}, f32[8,48,128]{2,1,0:T(8,128)}, f32[8,48,128]{2,1,0:T(8,128)}, f32[8,48,128]{2,1,0:T(8,128)}, f32[48,128]{1,0:T(8,128)}) custom-call(f32[8,48,128]{2,1,0:T(8,128)S(1)} %get-tuple-element.10.refs_0_, f32[8,48,128]{2,1,0:T(8,128)S(1)} %get-tuple-element.11.refs_1_, f32[8,48,128]{2,1,0:T(8,128)S(1)} %get-tuple-element.12.refs_2_, ...), custom_call_target="tpu_custom_call" | custom-call | tf_op jit(solution)/shard_map/pallas_call | solution.py:674
